TPU v7x, 256 devices: a whole 4x4x8 slice. The times are simulated.
256 devices in a mesh: group: 8 (over x, y_hi), tensor: 32 (over y_lo, z, core).
Axes of the slice: x: 4, y: 4 (y_hi: 2, y_lo: 2; y = y_hi * 2 + y_lo), z: 8, core: 2. Of those that a mesh axis runs over, the one named last changes fastest.
Arguments:
- learner_hidden_state: bfloat16 [32768, 8192], P(('group', 'tensor')), may hold values from -24 to 24
- learner_cotangent: bfloat16 [32768, 5120], P(('group', 'tensor')), may hold values from -24 to 24
- adapter_down_factor: float32 [8192, 64], P('tensor'), may hold values from -0.0625 to 0.0625
- adapter_up_factor: float32 [64, 5120], replicated, may hold values from -0.078125 to 0.078125
- output_projection: bfloat16 [8192, 5120], P('tensor'), may hold values from -0.0625 to 0.0625
- query_projection: bfloat16 [5120, 8192], P(None, 'tensor'), may hold values from -0.078125 to 0.078125
- key_projection: bfloat16 [5120, 1024], P(None, 'tensor'), may hold values from -0.15625 to 0.15625
- value_projection: bfloat16 [5120, 1024], P(None, 'tensor'), may hold values from -0.078125 to 0.078125
- decoder_layer_input: bfloat16 [4, 32, 5120], P(None, 'group'), may hold values from -6 to 6
- rotated_key_cache: bfloat16 [32, 4096, 1024], P('group', 'tensor'), may hold values from -720 to 720
- value_cache_store: bfloat16 [32, 4096, 1024], P('group', 'tensor'), may hold values from -16 to 16
- cache_fill_length: int32 [32], P('group'), may hold values from 1 to 4096, as said below
- rotary_start_position: int32 [32], P('group'), may hold values from 0 to 8191
- rollout_live_steps: int32 [32], P('group'), may hold values from 1 to 4, as said below
Outputs:
- decoded: bfloat16 [4, 32, 5120], P(None, 'group', 'tensor')
- fresh_down_factor: float32 [8192, 64], P('tensor')
- fresh_up_factor: float32 [64, 5120], P(None, ('group', 'tensor'))
Inputs may be any that keep to these rules, and one draw needn't show every extreme that they name: `cache_fill_length`: some rollout's cache holds all 4096 positions. `rollout_live_steps`: some rollout takes all 4 steps.
All inputs are finite; a program needn't handle non-finite values.
Results may differ from a plain program's by a relative error of at most 0.03.
Values may be sent and summed in bfloat16 or wider, within the bound.
A program may use at most 128 MiB of HBM per device.

v0:
```python
import math

import jax
import jax.numpy as jnp
from jax import lax
from jax.sharding import PartitionSpec as P

QH = 64
KVH = 8
HD = 128


adapter_scale = 0.01
rate_numerator = 50.0
rope_theta = 1000000.0
masked_score = -1e30


def joined(part, axis, combine):
    gathered = jax.tree.map(lambda a: lax.all_gather(a, axis), part)

    def take(source):
        return jax.tree.map(lambda a: lax.dynamic_index_in_dim(a, source, 0, False), gathered)

    return lax.fori_loop(
        1, lax.axis_size(axis), lambda source, state: combine(state, take(source)), take(0)
    )


def reduce_over_rows(left, right):
    return lax.dot_general(
        left, right, (((0,), (0,)), ((), ())), preferred_element_type=jnp.float32
    )


def rotate(vectors, positions):
    half = vectors.shape[-1] // 2
    freqs = jnp.exp(
        -math.log(rope_theta) * jnp.arange(half, dtype=jnp.float32) * (2.0 / vectors.shape[-1])
    )
    angles = positions.astype(jnp.float32)[..., None] * freqs
    cosine = jnp.concatenate([jnp.cos(angles)] * 2, axis=-1)[..., None, :]
    sine = jnp.concatenate([jnp.sin(angles)] * 2, axis=-1)[..., None, :]
    turned = jnp.concatenate([-vectors[..., half:], vectors[..., :half]], axis=-1)
    return vectors * cosine + turned * sine


def softmax_part(scores, valid):
    scores = jnp.where(valid, scores, masked_score)
    top = jnp.max(scores, axis=-1)
    weights = jnp.where(valid, jnp.exp(scores - top[..., None]), 0.0)
    return (top, weights)


def join_parts(first, second):
    peak = jnp.maximum(first[0], second[0])
    left = jnp.exp(first[0] - peak)
    right = jnp.exp(second[0] - peak)
    return (
        peak,
        first[1] * left + second[1] * right,
        first[2] * left[..., None] + second[2] * right[..., None],
    )


def body(
    learner_hidden_state,
    learner_cotangent,
    adapter_down_factor,
    adapter_up_factor,
    output_projection,
    query_projection,
    key_projection,
    value_projection,
    decoder_layer_input,
    rotated_key_cache,
    value_cache_store,
    cache_fill_length,
    rotary_start_position,
    rollout_live_steps,
):
    parts = lax.axis_size("tensor")
    column = lax.axis_index("tensor")
    slot = lax.axis_index("group") * parts + column
    tokens_all = learner_hidden_state.shape[0] * lax.axis_size("group") * parts
    step_rate = rate_numerator / math.sqrt(tokens_all)
    down_factor_slice = lax.all_gather(
        adapter_down_factor.astype(jnp.bfloat16), "tensor", axis=0, tiled=True
    )
    up_factor_slice = adapter_up_factor.astype(jnp.bfloat16)
    reduced_partial = jnp.dot(
        learner_hidden_state, down_factor_slice, preferred_element_type=jnp.float32
    ).astype(jnp.bfloat16)
    up_gradient = adapter_scale * reduce_over_rows(reduced_partial, learner_cotangent)
    backward_result = lax.dot_general(
        learner_cotangent,
        up_factor_slice,
        (((1,), (1,)), ((), ())),
        preferred_element_type=jnp.float32,
    ).astype(jnp.bfloat16)
    down_gradient = adapter_scale * reduce_over_rows(learner_hidden_state, backward_result)
    rows_per_shard = adapter_down_factor.shape[0]
    total_down, summed_up_gradient = lax.psum((down_gradient, up_gradient), ("group", "tensor"))
    fresh_down_factor = adapter_down_factor - step_rate * lax.dynamic_slice_in_dim(
        total_down, column * rows_per_shard, rows_per_shard, 0
    )
    complete_up_factor = adapter_up_factor - step_rate * summed_up_gradient
    cols_dev = complete_up_factor.shape[1] // (lax.axis_size("group") * parts)
    fresh_up_factor = lax.dynamic_slice_in_dim(complete_up_factor, slot * cols_dev, cols_dev, 1)
    up_merge = complete_up_factor.astype(jnp.bfloat16)
    merged_weight = (
        output_projection.astype(jnp.float32)
        + adapter_scale
        * jnp.dot(
            fresh_down_factor.astype(jnp.bfloat16), up_merge, preferred_element_type=jnp.float32
        )
    ).astype(jnp.bfloat16)
    steps, roll, width = decoder_layer_input.shape
    flat = decoder_layer_input.reshape(steps * roll, width)
    query_part = jnp.dot(flat, query_projection, preferred_element_type=jnp.float32).astype(
        jnp.bfloat16
    )
    key_part = jnp.dot(flat, key_projection, preferred_element_type=jnp.float32).astype(
        jnp.bfloat16
    )
    value_part = jnp.dot(flat, value_projection, preferred_element_type=jnp.float32).astype(
        jnp.bfloat16
    )
    queries, new_keys, new_values = (
        lax.all_gather(query_part, "tensor", axis=1, tiled=True),
        lax.all_gather(key_part, "tensor", axis=1, tiled=True),
        lax.all_gather(value_part, "tensor", axis=1, tiled=True),
    )
    group_size = QH // KVH
    order = jnp.arange(steps, dtype=jnp.int32)
    positions = rotary_start_position[None, :] + order[:, None]
    queries = rotate(queries.reshape(steps, roll, QH, HD).astype(jnp.float32), positions).astype(
        jnp.bfloat16
    )
    queries = queries.reshape(steps, roll, KVH, group_size, HD)
    new_keys = rotate(new_keys.reshape(steps, roll, KVH, HD).astype(jnp.float32), positions).astype(
        jnp.bfloat16
    )
    new_values = new_values.reshape(steps, roll, KVH, HD)
    inv_root = 1.0 / math.sqrt(HD)
    context = rotated_key_cache.shape[1]
    cached_k = rotated_key_cache.reshape(roll, context, KVH, HD)
    cached_v = value_cache_store.reshape(roll, context, KVH, HD)
    spots = column * context + jnp.arange(context, dtype=jnp.int32)
    cache_valid = (spots[None, :] < cache_fill_length[:, None])[None, :, None, None, :]
    scores = (
        jnp.einsum("srkgd,rckd->srkgc", queries, cached_k, preferred_element_type=jnp.float32)
        * inv_root
    )
    cache_top, cache_weights = softmax_part(scores, cache_valid)
    cache_total = jnp.sum(cache_weights, axis=-1).reshape(steps, roll, QH)
    cache_acc = jnp.einsum(
        "srkgc,rckd->srkgd", cache_weights, cached_v.astype(jnp.float32)
    ).reshape(steps, roll, QH, HD)
    cache_top = cache_top.reshape(steps, roll, QH)
    new_scores = (
        jnp.einsum("srkgd,trkd->srkgt", queries, new_keys, preferred_element_type=jnp.float32)
        * inv_root
    )
    new_valid = (order[None, :] <= order[:, None])[:, None, None, None, :]
    new_top, new_weights = softmax_part(new_scores, new_valid)
    new_total = jnp.sum(new_weights, axis=-1).reshape(steps, roll, QH)
    new_acc = jnp.einsum("srkgt,trkd->srkgd", new_weights, new_values.astype(jnp.float32)).reshape(
        steps, roll, QH, HD
    )
    new_top = new_top.reshape(steps, roll, QH)
    heads_dev = QH // parts
    first_head = column * heads_dev
    top, total, acc = joined((cache_top, cache_total, cache_acc), "tensor", join_parts)
    top = lax.dynamic_slice_in_dim(top, first_head, heads_dev, 2)
    total = lax.dynamic_slice_in_dim(total, first_head, heads_dev, 2)
    acc = lax.dynamic_slice_in_dim(acc, first_head, heads_dev, 2)
    own_top = lax.dynamic_slice_in_dim(new_top, first_head, heads_dev, 2)
    own_total = lax.dynamic_slice_in_dim(new_total, first_head, heads_dev, 2)
    own_acc = lax.dynamic_slice_in_dim(new_acc, first_head, heads_dev, 2)
    peak = jnp.maximum(top, own_top)
    left = jnp.exp(top - peak)
    right = jnp.exp(own_top - peak)
    heads_out = (acc * left[..., None] + own_acc * right[..., None]) / (
        total * left + own_total * right
    )[..., None]
    heads_out = heads_out.astype(jnp.bfloat16).reshape(steps * roll, heads_dev * HD)
    partial_value = jnp.dot(heads_out, merged_weight, preferred_element_type=jnp.float32)
    shared = lax.psum_scatter(
        partial_value.astype(jnp.bfloat16), "tensor", scatter_dimension=1, tiled=True
    ).astype(jnp.float32)
    live = (order[:, None] < rollout_live_steps[None, :]).reshape(steps * roll, 1)
    decoded = (
        jnp.where(live, shared, 0.0).astype(jnp.bfloat16).reshape(steps, roll, shared.shape[1])
    )
    return (decoded, fresh_down_factor, fresh_up_factor)


def solution(mesh):
    return jax.shard_map(
        body,
        mesh=mesh,
        in_specs=(
            P(("group", "tensor"), None),
            P(("group", "tensor"), None),
            P("tensor", None),
            P(),
            P("tensor", None),
            P(None, "tensor"),
            P(None, "tensor"),
            P(None, "tensor"),
            P(None, "group", None),
            P("group", "tensor", None),
            P("group", "tensor", None),
            P("group"),
            P("group"),
            P("group"),
        ),
        out_specs=(P(None, "group", "tensor"), P("tensor", None), P(None, ("group", "tensor"))),
        check_vma=False,
    )
```

profile of v0, /device:TPU:3, one launch (start us, length us, event | category | flops | bytes accessed | tf_op | source)
XLA Modules:
  0.0 646.9 jit_solution(10087723212020802060)
XLA Ops:
  7.2 1.6 convert_element_type.97
  10.3 38.5 %all_gather.21 = bf16[16,8192]{1,0:T(8,128)(2,1)S(1)} all-gather(bf16[16,256]{1,0:T(8,128)(2,1)S(1)} %convolution_convert_fusion.3), channel_id=1, replica_groups=mesh['group'=8,'tensor'=32] {'tensor'}, dimensions={1}, use_global_device_ids=true | all-gather | bytes 270336 | tf_op jit(solution)/shard_map/all_gather | solution.py:130
  49.0 2.6 copy.80
  53.1 5.2 fusion.3
  58.3 18.0 %all-gather.7.cloned.1.call-done = bf16[8192,64]{0,1:T(8,128)(2,1)} async-done(((bf16[256,64]{0,1:T(8,128)(2,1)}), bf16[8192,64]{0,1:T(8,128)(2,1)}) %all-gather.7.cloned.1.call-update) | async-done | bytes 1048592 | tf_op jit(solution)/shard_map/all_gather | solution.py:87
  76.3 4.8 convolution_multiply_fusion.2
  86.5 33.0 %all-gather = bf16[32,32,16]{1,2,0:T(8,128)(2,1)S(1)} all-gather(bf16[1,32,16]{1,2,0:T(8,128)(2,1)S(1)} %fusion.10), channel_id=1, replica_groups=mesh['group'=8,'tensor'=32] {'tensor'}, dimensions={0}, use_global_device_ids=true | all-gather | bytes 33792 | tf_op jit(solution)/shard_map/all_gather | solution.py:131
  124.0 31.1 %all-gather.1 = bf16[32,32,16]{1,2,0:T(8,128)(2,1)S(1)} all-gather(bf16[1,32,16]{1,2,0:T(8,128)(2,1)S(1)} %fusion.11), channel_id=1, replica_groups=mesh['group'=8,'tensor'=32] {'tensor'}, dimensions={0}, use_global_device_ids=true | all-gather | bytes 33792 | tf_op jit(solution)/shard_map/all_gather | solution.py:132
  156.5 32.7 %all_gather.23 = f32[32,4,4,64]{3,2,1,0:T(4,128)S(1)} all-gather(f32[1,4,4,64]{3,2,1,0:T(4,128)S(1)} %all_gather_reshape.10), channel_id=1, replica_groups=mesh['group'=8,'tensor'=32] {'tensor'}, dimensions={0}, use_global_device_ids=true | all-gather | bytes 135168 | tf_op jit(solution)/shard_map/all_gather | solution.py:20
  189.2 31.4 %all_gather.22 = f32[32,4,4,64]{3,2,1,0:T(4,128)S(1)} all-gather(f32[1,4,4,64]{3,2,1,0:T(4,128)S(1)} %all_gather_reshape.9), channel_id=1, replica_groups=mesh['group'=8,'tensor'=32] {'tensor'}, dimensions={0}, use_global_device_ids=true | all-gather | bytes 135168 | tf_op jit(solution)/shard_map/all_gather | solution.py:20
  221.4 122.9 %all-reduce.3.cloned.1.call-done = (f32[64,5120]{1,0:T(8,128)}, f32[8192,64]{0,1:T(8,128)}) async-done(((f32[64,5120]{1,0:T(8,128)}, f32[8192,64]{0,1:T(8,128)}), (f32[64,5120]{1,0:T(8,128)}, f32[8192,64]{0,1:T(8,128)})) %all-reduce.3.cloned.1.call-update) | async-done | bytes 3407888 | tf_op jit(solution)/shard_map/psum | solution.py:103
  345.1 3.0 multiply_subtract_fusion
  348.1 98.7 %all-gather.5.cloned.1.call-done = f32[32,4,4,64,128]{4,3,2,1,0:T(8,128)} async-done(((f32[1,4,4,64,128]{4,3,2,1,0:T(8,128)}), f32[32,4,4,64,128]{4,3,2,1,0:T(8,128)}) %all-gather.5.cloned.1.call-update) | async-done | bytes 16777232 | tf_op jit(solution)/shard_map/all_gather | solution.py:20
  447.9 71.2 %while.19 = (s32[]{:T(128)}, f32[4,4,64]{2,1,0:T(4,128)S(1)}, f32[4,4,64]{2,1,0:T(4,128)S(1)}, f32[4,4,64,128]{3,2,1,0:T(8,128)S(1)}, f32[32,4,4,64]{3,2,1,0:T(4...) while((s32[]{:T(128)}, f32[4,4,64]{2,1,0:T(4,128)S(1)}, ...), condition=%wide.region_3.4_spmd, body=%wide.region_2.3_spmd.sunk | while | flops 399365 | bytes 1613975 | solution.py:25
  448.7 1.5 fusion.65
  451.0 1.5 fusion.65
  453.3 1.5 fusion.65
  455.6 1.5 fusion.65
  457.9 1.5 fusion.65
  460.2 1.5 fusion.65
  462.4 1.5 fusion.65
  464.7 1.5 fusion.65
  467.0 1.5 fusion.65
  469.3 1.5 fusion.65
  471.6 1.5 fusion.65
  473.9 1.5 fusion.65
  476.2 1.5 fusion.65
  478.5 1.5 fusion.65
  487.7 1.5 fusion.65
  515.3 1.5 fusion.65
  520.2 3.3 convolution_convert_fusion
  526.8 112.0 %reduce-scatter.4.cloned.1.call-done = bf16[160,16]{1,0:T(8,128)(2,1)} async-done(((bf16[5120,16]{1,0:T(8,128)(2,1)}), bf16[160,16]{1,0:T(8,128)(2,1)}) %reduce-scatter.4.cloned.1.call-update) | async-done | bytes 5136
  (138 shorter events, 68.6 us)
Async XLA Ops:
  7.2 2.7 copy-start
  7.2 69.1 %all-gather.7.cloned.1.call-start = ((), (), s32[]{:S(2)}) async-start(), calls=%async_computation.2 | async-start | bytes 1081344 | tf_op jit(solution)/shard_map/all_gather | solution.py:87
  8.9 335.4 %all-reduce.3.cloned.1.call-start = ((), (), s32[]{:S(2)}) async-start(), calls=%async_computation.4 | async-start | bytes 6815744 | tf_op jit(solution)/shard_map/psum | solution.py:103
  49.0 2.6 copy-start.3
  49.0 3.9 copy-start.12
  49.0 4.0 copy-start.11
  81.1 365.7 %all-gather.5.cloned.1.call-start = ((), (), s32[]{:S(2)}) async-start(), calls=%async_computation.1 | async-start | bytes 17301504 | tf_op jit(solution)/shard_map/all_gather | solution.py:20
  81.1 1.2 copy-start.2
  81.7 1.6 copy-start.4
  81.7 1.5 copy-start.1
  84.6 554.2 %reduce-scatter.4.cloned.1.call-start = ((), (), s32[]{:S(2)}) async-start(), calls=%async_computation.3 | async-start | bytes 1351680
  85.1 34.7 %copy-start.5 = (bf16[4,4,8,8,128]{4,3,2,1,0:T(8,128)(2,1)S(1)}, bf16[4,4,8,8,128]{4,3,2,1,0:T(8,128)(2,1)}, u32[]{:S(2)}) copy-start(bf16[4,4,8,8,128]{4,3,2,1,0:T(8,128)(2,1)} %copy-done.4) | copy-start | bytes 786436
  121.2 223.1 %copy-start.8 = (f32[256,64]{0,1:T(8,128)S(1)}, f32[256,64]{0,1:T(8,128)}, u32[]{:S(2)}) copy-start(f32[256,64]{0,1:T(8,128)} %param.18) | copy-start | bytes 196612
  220.6 0.7 copy-start.6
  345.1 175.1 %copy-start.7 = (f32[256,64]{0,1:T(8,128)}, f32[256,64]{0,1:T(8,128)S(1)}, u32[]{:S(2)}) copy-start(f32[256,64]{0,1:T(8,128)S(1)} %multiply_subtract_fusion.1) | copy-start | bytes 196612
  447.9 71.3 %copy-start.9 = (f32[4,4,64]{2,1,0:T(4,128)S(1)}, f32[4,4,64]{2,1,0:T(4,128)}, u32[]{:S(2)}) copy-start(f32[4,4,64]{2,1,0:T(4,128)} %reshape.141) | copy-start | bytes 12292
  447.9 71.2 %copy-start.10 = (f32[4,4,64]{2,1,0:T(4,128)S(1)}, f32[4,4,64]{2,1,0:T(4,128)}, u32[]{:S(2)}) copy-start(f32[4,4,64]{2,1,0:T(4,128)} %reshape.138) | copy-start | bytes 12292
  523.6 1.5 copy-start.13
Sparse Core Ops, SparseCore 0:
  10.4 65.9 all-gather.6
  82.0 262.1 all-reduce.2
  346.3 100.4 all-gather.4
  525.2 113.5 reduce-scatter.3
where the time goes:
time: 654 us; the launch traced here: 647 us
  waiting for transfers between devices  352 us (54%)
  blocking collectives  167 us (26%)
  other arithmetic  78.7 us (12%)
  matrix products  18.9 us (3%)
  local copies, waits for them, and re-layouts  16 us (2%)
  between operations  14.1 us (2%)
    psum x1, waiting for transfers between devices, body(): lax.psum((down_gradient, up_gradient), ('group', 'tensor'))  123 us
    unnamed x5, waiting for transfers between devices  112 us
    all_gather x1, waiting for transfers between devices, joined(): gathered = jax.tree.map(lambda a: lax.all_gather(a, axis), part)  98.7 us
    all_gather x2, blocking collectives, joined(): gathered = jax.tree.map(lambda a: lax.all_gather(a, axis), part)  64.1 us
    add x31, other arithmetic, join_parts(): first[2] * left[..., None] + second[2] * right[..., None]  48 us
    all_gather x1, blocking collectives, body(): lax.all_gather(query_part, 'tensor', axis=1, tiled=True)  38.5 us
    all_gather x1, blocking collectives, body(): lax.all_gather(key_part, 'tensor', axis=1, tiled=True)  33 us
    all_gather x1, blocking collectives, body(): lax.all_gather(value_part, 'tensor', axis=1, tiled=True)  31.1 us
  transfers between devices with their start and end apart: 4, of which 4 were waited for; matrix products, arithmetic and copies ran while one was open for 4% of the time, Pallas kernels for 0%

commit v1 on v0

v1 whole, which is shorter than its diff:
```python
import math

import jax
import jax.numpy as jnp
from jax import lax
from jax.experimental import pallas as pl
from jax.experimental.pallas import tpu as pltpu
from jax.sharding import PartitionSpec as P

MESH = pl.DeviceIdType.MESH
F32 = jnp.float32
BF16 = jnp.bfloat16

adapter_scale = 0.01
rate_numerator = 50.0
rope_theta = 1000000.0
masked_score = -1e30

HD = 128
TOKENS = 32768
STEP_SCALE = adapter_scale * rate_numerator / math.sqrt(TOKENS)
INV_ROOT = 1.0 / math.sqrt(HD)

NN = (((1,), (0,)), ((), ()))
NT = (((1,), (1,)), ((), ()))


def dot(a, b, dims=NN):
    return lax.dot_general(a, b, dims, preferred_element_type=F32)


def rcopy(src, dst, ss, rs, dev):
    return pltpu.make_async_remote_copy(
        src_ref=src, dst_ref=dst, send_sem=ss, recv_sem=rs, device_id=dev, device_id_type=MESH
    )


def loop(n, fn, start=0):
    def step(k, carry):
        fn(k)
        return carry

    lax.fori_loop(start, n, step, 0)


SCRATCH = dict(
    v_down=((64, 256), F32),
    v_x=((4, 4, 5120), BF16),
    x_rows=((16, 5120), F32),
    v_wq=((5120, 256), BF16),
    v_wkv=((64, 5120), BF16),
    v_up=((64, 5120), F32),
    v_cot=((128, 5120), BF16),
    v_hid=((128, 8192), BF16),
    v_wo=((256, 5120), BF16),
    kbuf=((2, 4, 128, 512), BF16),
    vbuf=((2, 4, 128, 512), BF16),
    down_all=((32, 64, 256), BF16),
    q_rot0=((16, 128), F32),
    q_rot1=((16, 128), F32),
    q_rows=((32, 128), F32),
    q_send=((32, 128), BF16),
    q_buf=((16, 32, 128), BF16),
    n_buf=((4, 16, 128), BF16),
    n_send=((16, 128), BF16),
    a_send=((16, 32, 128), BF16),
    a_recv=((16, 32, 128), BF16),
    l_send=((16, 8, 128), F32),
    l_recv=((16, 8, 128), F32),
    g_send1=((2, 16, 64, 256), BF16),
    g_keep=((2, 16, 64, 256), F32),
    g_recv1=((2, 16, 64, 256), BF16),
    g_send2=((2, 8, 128, 256), BF16),
    g_recv2=((2, 8, 128, 256), BF16),
    g_send3=((2, 16, 16, 128), BF16),
    g_recv3=((2, 16, 16, 128), BF16),
    g_send4=((2, 16, 128), F32),
    g_recv4=((2, 8, 16, 128), F32),
    u_tmp=((64, 1280), F32),
    p_rows=((16, 5120), F32),
    fd_pad=((128, 256), BF16),
    fu_pad=((128, 256), BF16),
    fu_rows=((256, 128), F32),
    o_send1=((16, 16, 256), BF16),
    o_keep=((16, 16, 256), F32),
    o_recv1=((16, 16, 256), BF16),
    o_send2=((16, 16, 256), BF16),
    o_recv2=((16, 16, 256), BF16),
    d_rows=((16, 256), F32),
    f_send=((8, 24, 128), F32),
    f_recv=((24, 128), F32),
)
SEMS = dict(
    load=(12,),
    dn_sz=(8,),
    dn_sy=(8,),
    dn_sc=(16,),
    dn_r=(32,),
    kv_s=(2,),
    kv_r=(2,),
    q_s=(16,),
    q_r=(16,),
    n_s=(4,),
    n_r=(4,),
    a_s=(16,),
    a_r=(16,),
    l_s=(16,),
    l_r=(16,),
    g1_s=(2, 4),
    g1_r=(2, 4),
    g2_s=(2, 8),
    g2_r=(2, 8),
    g3_s=(2, 16),
    g3_r=(2, 16),
    g4_s=(2, 8),
    g4_r=(2, 8),
    o1_s=(1,),
    o1_r=(1,),
    o2_s=(16,),
    o2_r=(16,),
    f_s=(8,),
    f_r=(1,),
)


class Names:
    pass


def lanes(shape):
    return lax.broadcasted_iota(jnp.int32, shape, len(shape) - 1)


def sublanes(shape):
    return lax.broadcasted_iota(jnp.int32, shape, len(shape) - 2)


def by_rollout(rollout, ref):
    picked = jnp.where(rollout == 0, ref[0], ref[1])
    picked = jnp.where(rollout == 2, ref[2], picked)
    return jnp.where(rollout == 3, ref[3], picked)


def kernel(
    hid, cot, down, up, wo, wq, wk, wv, x, kc, vc, fill, start, live, dec_out, fd_out, fu_out, *refs
):
    n = Names()
    for name, ref in zip(list(SCRATCH) + ["s_" + key for key in SEMS], refs):
        setattr(n, name, ref)
    t = lax.axis_index("tensor")
    g = lax.axis_index("group")
    c = lax.rem(t, 2)
    i0 = lax.div(t, 2)
    y = lax.div(t, 16)
    z = lax.rem(i0, 8)
    t16 = lax.rem(t, 16)
    sib = {"tensor": t + 1 - 2 * c}
    ypart = {"tensor": lax.rem(t + 16, 32)}

    def tdev(index):
        return {"tensor": index}

    def gdev(index):
        return {"group": index}

    barrier = pltpu.get_barrier_semaphore()
    loop(
        32,
        lambda k: pl.semaphore_signal(
            barrier, inc=1, device_id=tdev(lax.rem(t + k, 32)), device_id_type=MESH
        ),
        1,
    )
    loop(
        8,
        lambda k: pl.semaphore_signal(
            barrier, inc=1, device_id=gdev(lax.rem(g + k, 8)), device_id_type=MESH
        ),
        1,
    )

    own_half = pl.ds(pl.multiple_of(512 * c, 512), 512)
    sib_half = pl.ds(pl.multiple_of(512 * (1 - c), 512), 512)
    loads = dict(
        down=(down, n.v_down),
        x=(x, n.v_x),
        wq=(wq, n.v_wq),
        wk=(wk, n.v_wkv.at[pl.ds(0, 32)]),
        wv=(wv, n.v_wkv.at[pl.ds(32, 32)]),
        up=(up, n.v_up),
        cot=(cot, n.v_cot),
        hid=(hid, n.v_hid),
        k=(kc.at[:, :, own_half], n.kbuf.at[0]),
        v=(vc.at[:, :, own_half], n.vbuf.at[0]),
        wo=(wo, n.v_wo),
    )
    loads = {
        key: pltpu.make_async_copy(src, dst, n.s_load.at[at])
        for at, (key, (src, dst)) in enumerate(loads.items())
    }
    for copy in loads.values():
        copy.start()

    loads["down"].wait()
    n.down_all[t] = n.v_down[...].astype(BF16)

    pl.semaphore_wait(barrier, 38)

    def dn(slot, ss, dev):
        return rcopy(n.down_all.at[slot], n.down_all.at[slot], ss, n.s_dn_r.at[slot], dev)

    def dn_z(k):
        to = y * 16 + lax.rem(z + k, 8) * 2 + c
        return dn(t, n.s_dn_sz.at[k], tdev(to))

    def dn_y(k):
        slot = y * 16 + lax.rem(z + k, 8) * 2 + c
        return dn(slot, n.s_dn_sy.at[k], ypart)

    def dn_c(k):
        slot = lax.rem(y + lax.div(k, 8), 2) * 16 + lax.rem(z + k, 8) * 2 + c
        return dn(slot, n.s_dn_sc.at[k], sib)

    loop(8, lambda k: dn_z(k).start(), 1)
    dn_y(0).start()
    dn_c(0).start()

    kv = [
        rcopy(src.at[:, :, sib_half], dst.at[1], n.s_kv_s.at[at], n.s_kv_r.at[at], sib)
        for at, (src, dst) in enumerate(((kc, n.kbuf), (vc, n.vbuf)))
    ]
    for copy in kv:
        copy.start()

    loads["x"].wait()
    for s in range(4):
        n.x_rows[s * 4 : s * 4 + 4, :] = n.v_x[s].astype(F32)
    xb = n.x_rows[...].astype(BF16)
    row = sublanes((16, HD))
    lane = lanes((16, HD))
    position = (by_rollout(row & 3, start) + (row >> 2)).astype(F32)
    freq = jnp.exp((lane & 63).astype(F32) * (-math.log(rope_theta) * 2.0 / HD))
    angle = position * freq
    cosine = jnp.cos(angle)
    sine = jnp.where(lane < 64, -jnp.sin(angle), jnp.sin(angle))

    def rotate(v):
        v = v.astype(BF16).astype(F32)
        return v * cosine + pltpu.roll(v, 64, 1) * sine

    loads["wq"].wait()
    q = dot(xb, n.v_wq[...])
    for h, rows in enumerate((n.q_rot0, n.q_rot1)):
        rows[...] = rotate(q[:, h * HD : (h + 1) * HD])
        for r in range(4):
            n.q_rows[r * 8 + h * 4 : r * 8 + h * 4 + 4, :] = rows[pl.ds(r, 4, stride=4), :]
    n.q_send[...] = n.q_rows[...].astype(BF16)

    def q_copy(k):
        i = lax.rem(i0 + k, 16)
        return rcopy(n.q_send, n.q_buf.at[t16], n.s_q_s.at[k], n.s_q_r.at[t16], tdev(2 * i + y))

    @pl.when(c != y)
    def _():
        q_copy(0).start()

    loop(16, lambda k: q_copy(k).start(), 1)

    @pl.when(c == y)
    def _():
        n.q_buf[t16] = n.q_send[...]

    loads["wk"].wait()
    loads["wv"].wait()
    nkv = dot(xb, n.v_wkv[...], NT)
    n.n_send[...] = jnp.concatenate([nkv, nkv], axis=1).astype(BF16)
    b4 = lax.rem(t, 4)

    def n_copy(k):
        to = t - b4 + lax.rem(b4 + k, 4)
        return rcopy(n.n_send, n.n_buf.at[b4], n.s_n_s.at[k], n.s_n_r.at[b4], tdev(to))

    loop(4, lambda k: n_copy(k).start(), 1)
    n.n_buf[b4] = n.n_send[...]

    def g1(u, part):
        at = pl.ds(part * 4, 4)
        return rcopy(
            n.g_send1.at[u, at], n.g_recv1.at[u, at], n.s_g1_s.at[u, part], n.s_g1_r.at[u, part], sib
        )

    def g2(u, k):
        j = lax.rem(g + k, 8)
        return rcopy(
            n.g_send2.at[u, j], n.g_recv2.at[u, g], n.s_g2_s.at[u, k], n.s_g2_r.at[u, g], gdev(j)
        )

    def g2_in(u, k):
        j = lax.rem(g + k, 8)
        return rcopy(
            n.g_send2.at[u, j], n.g_recv2.at[u, j], n.s_g2_s.at[u, k], n.s_g2_r.at[u, j], gdev(j)
        )

    def g3(u, k):
        i = lax.rem(i0 + k, 16)
        return rcopy(
            n.g_send3.at[u, i], n.g_recv3.at[u, i0], n.s_g3_s.at[u, k], n.s_g3_r.at[u, i0],
            tdev(2 * i + c),
        )

    def g3_in(u, k):
        i = lax.rem(i0 + k, 16)
        return rcopy(
            n.g_send3.at[u, i], n.g_recv3.at[u, i], n.s_g3_s.at[u, k], n.s_g3_r.at[u, i],
            tdev(2 * i + c),
        )

    def g4(u, k):
        j = lax.rem(g + k, 8)
        return rcopy(
            n.g_send4.at[u], n.g_recv4.at[u, g], n.s_g4_s.at[u, k], n.s_g4_r.at[u, g], gdev(j)
        )

    def g4_in(u, k):
        j = lax.rem(g + k, 8)
        return rcopy(
            n.g_send4.at[u], n.g_recv4.at[u, j], n.s_g4_s.at[u, k], n.s_g4_r.at[u, j], gdev(j)
        )

    def stage2_out(u):
        def part_sum(part):
            g1(u, part).wait_recv()
            for pair in range(2):
                at = part * 4 + pair * 2
                first = n.g_keep[u, at] + n.g_recv1[u, at].astype(F32)
                second = n.g_keep[u, at + 1] + n.g_recv1[u, at + 1].astype(F32)
                rows = pl.ds(pl.multiple_of(at * 8, 16), 16)
                for j in range(8):
                    both = jnp.concatenate(
                        [first[j * 8 : j * 8 + 8], second[j * 8 : j * 8 + 8]], axis=0
                    )
                    n.g_send2[u, j, rows, :] = both.astype(BF16)

        loop(4, part_sum)
        loop(8, lambda k: g2(u, k).start(), 1)

    def stage3_out(u):
        loop(8, lambda k: g2_in(u, k).wait_recv(), 1)
        n.g_recv2[u, g] = n.g_send2[u, g]

        def pair_sum(pair):
            rows = pl.ds(pl.multiple_of(pair * 16, 16), 16)
            total = n.g_recv2[u, 0, rows, :].astype(F32)
            for j in range(1, 8):
                total = total + n.g_recv2[u, j, rows, :].astype(F32)
            for e in range(2):
                piece = total[e * 8 : e * 8 + 8]
                n.g_send3[u, pair * 2 + e] = jnp.concatenate(
                    [piece[:, :128], piece[:, 128:]], axis=0
                ).astype(BF16)

        loop(8, pair_sum)
        loop(16, lambda k: g3(u, k).start(), 1)

    def stage4_out(u):
        loop(16, lambda k: g3_in(u, k).wait_recv(), 1)
        n.g_recv3[u, i0] = n.g_send3[u, i0]
        total = n.g_recv3[u, 0].astype(F32)
        for i in range(1, 16):
            total = total + n.g_recv3[u, i].astype(F32)
        n.g_send4[u] = total
        n.g_recv4[u, g] = total
        loop(8, lambda k: g4(u, k).start(), 1)

    def summed(u):
        loop(8, lambda k: g4_in(u, k).wait_recv(), 1)
        pieces = [n.g_recv4[u, j] for j in range(8)]
        return jnp.concatenate(
            [jnp.concatenate([p[:8], p[8:]], axis=1) for p in pieces], axis=0
        )

    loads["up"].wait()
    loads["cot"].wait()
    back = dot(n.v_up[...].astype(BF16), n.v_cot[...], NT).astype(BF16)
    loads["hid"].wait()

    def down_part(part):
        for e in range(4):
            i = part * 4 + e
            at = pl.multiple_of((2 * i + 1 - c) * 256, 256)
            n.g_send1[0, i] = dot(back, n.v_hid[:, pl.ds(at, 256)]).astype(BF16)
        g1(0, part).start()
        for e in range(4):
            i = part * 4 + e
            at = pl.multiple_of((2 * i + c) * 256, 256)
            n.g_keep[0, i] = dot(back, n.v_hid[:, pl.ds(at, 256)])

    loop(4, down_part)

    def pass_z(k):
        slot = y * 16 + lax.rem(z + k, 8) * 2 + c
        dn(slot, n.s_dn_sz.at[k], sib).wait_recv()
        dn_y(k).start()
        dn_c(k).start()

    loop(8, pass_z, 1)

    stage2_out(0)

    def pass_y(k):
        dn_c(k).wait_recv()
        dn_c(k).start()

    loop(16, pass_y, 8)

    def q_in(k):
        i = lax.rem(t16 + k, 16)
        return rcopy(n.q_send, n.q_buf.at[i], n.s_q_s.at[k], n.s_q_r.at[i], sib)

    @pl.when(c != y)
    def _():
        q_in(0).wait_recv()

    loop(16, lambda k: q_in(k).wait_recv(), 1)
    loads["k"].wait()
    loads["v"].wait()
    for copy in kv:
        copy.wait_recv()

    spot = lanes((32, 256))
    spot = jnp.where(spot < 128, t * 128 + spot, (t + 1 - 2 * c) * 128 + spot - 128)
    tile_lane = lanes((8, 128))

    def attend(kk):
        cols = pl.ds(pl.multiple_of(kk * HD, HD), HD)
        qs = [n.q_buf[kk * 4 + j].astype(F32) for j in range(4)]
        outs, tops, sums = [], [], []
        for r in range(4):
            qr = jnp.concatenate([a[r * 8 : r * 8 + 8] for a in qs], axis=0).astype(BF16)
            keys = jnp.concatenate([n.kbuf[0, r, :, cols], n.kbuf[1, r, :, cols]], axis=0)
            values = jnp.concatenate([n.vbuf[0, r, :, cols], n.vbuf[1, r, :, cols]], axis=0)
            valid = spot < fill[r]
            scores = jnp.where(valid, dot(qr, keys, NT) * INV_ROOT, masked_score)
            top = jnp.max(scores, axis=1, keepdims=True)
            weights = jnp.where(valid, jnp.exp(scores - top), 0.0)
            tops.append(top)
            sums.append(jnp.sum(weights, axis=1, keepdims=True))
            outs.append(dot(weights.astype(BF16), values))
        for j in range(4):
            rows = slice(j * 8, j * 8 + 8)
            n.a_send[kk * 4 + j] = jnp.concatenate([o[rows] for o in outs], axis=0).astype(BF16)
            tile = jnp.zeros((8, 128), F32)
            for r in range(4):
                tile = jnp.where(tile_lane == r, tops[r][rows], tile)
                tile = jnp.where(tile_lane == 64 + r, sums[r][rows], tile)
            n.l_send[kk * 4 + j] = tile

    loop(4, attend)

    def a_copy(k):
        i = lax.rem(t16 + k, 16)
        to = tdev(16 * c + i)
        return (
            rcopy(n.a_send.at[i], n.a_recv.at[i0], n.s_a_s.at[k], n.s_a_r.at[i0], to),
            rcopy(n.l_send.at[i], n.l_recv.at[i0], n.s_l_s.at[k], n.s_l_r.at[i0], to),
        )

    def a_start(k):
        for copy in a_copy(k):
            copy.start()

    @pl.when(c != y)
    def _():
        a_start(0)

    loop(16, a_start, 1)

    @pl.when(c == y)
    def _():
        n.a_recv[i0] = n.a_send[t16]
        n.l_recv[i0] = n.l_send[t16]

    def dn_in(k):
        slot = lax.rem(y + lax.div(k, 8), 2) * 16 + lax.rem(z + k, 8) * 2 + 1 - c
        dn(slot, n.s_dn_sc.at[k], sib).wait_recv()

    loop(16, dn_in)

    def reduce_part(part, total):
        for e in range(4):
            at = part * 4 + e
            cols = pl.ds(pl.multiple_of(at * 256, 256), 256)
            total = total + dot(n.down_all[at], n.v_hid[:, cols], NT)
        return total

    reduced = lax.fori_loop(0, 8, reduce_part, jnp.zeros((64, 128), F32)).astype(BF16)

    def up_part(part):
        n.u_tmp[...] = dot(reduced, n.v_cot[:, pl.ds(pl.multiple_of(part * 1280, 1280), 1280)])
        for pair in range(4):
            both = []
            for e in (pair * 2, pair * 2 + 1):
                at = 160 * e // 128 * 128
                shift = 160 * e - at
                window = n.u_tmp[:, at : at + 256]
                both.append(pltpu.roll(window, 256 - shift, 1) if shift else window)
            n.g_send1[1, part * 4 + pair] = jnp.where(c == 0, both[1], both[0]).astype(BF16)
            n.g_keep[1, part * 4 + pair] = jnp.where(c == 0, both[0], both[1])
        g1(1, part).start()

    loop(4, up_part)

    stage3_out(0)
    stage2_out(1)

    loop(4, lambda k: rcopy(
        n.n_send, n.n_buf.at[lax.rem(b4 + k, 4)], n.s_n_s.at[k], n.s_n_r.at[lax.rem(b4 + k, 4)], sib
    ).wait_recv(), 1)
    fresh = [n.n_buf[j].astype(F32) for j in range(4)]
    quarter = lane >> 5
    new_k = fresh[0]
    new_v = pltpu.roll(fresh[0], 96, 1)
    for j in range(1, 4):
        new_k = jnp.where(quarter == j, pltpu.roll(fresh[j], 32 * j, 1), new_k)
        new_v = jnp.where(quarter == j, pltpu.roll(fresh[j], (32 * j + 96) % 128, 1), new_v)
    new_k = rotate(new_k).astype(BF16)
    new_v = new_v.astype(BF16)
    nrow = sublanes((32, 16))
    ncol = lanes((32, 16))
    new_valid = ((nrow >> 3) == (ncol & 3)) & ((ncol >> 2) <= (nrow & 3))
    new_scores = jnp.where(new_valid, dot(n.q_send[...], new_k, NT) * INV_ROOT, masked_score)
    new_top = jnp.max(new_scores, axis=1, keepdims=True)
    new_weights = jnp.where(new_valid, jnp.exp(new_scores - new_top), 0.0)
    new_sum = jnp.sum(new_weights, axis=1, keepdims=True)
    new_out = dot(new_weights.astype(BF16), new_v)
    new_tile = jnp.zeros((8, 128), F32)
    new_total = jnp.zeros((8, 128), F32)
    for r in range(4):
        rows = slice(r * 8, r * 8 + 8)
        new_tile = jnp.where(tile_lane == r, new_top[rows], new_tile)
        new_total = jnp.where(tile_lane == r, new_sum[rows], new_total)

    def a_in(k):
        i = lax.rem(i0 + k, 16)
        rcopy(n.a_send.at[0], n.a_recv.at[i], n.s_a_s.at[k], n.s_a_r.at[i], sib).wait_recv()
        rcopy(n.l_send.at[0], n.l_recv.at[i], n.s_l_s.at[k], n.s_l_r.at[i], sib).wait_recv()

    @pl.when(c != y)
    def _():
        a_in(0)

    loop(16, a_in, 1)

    peak = lax.fori_loop(0, 16, lambda i, m: jnp.maximum(m, n.l_recv[i]), new_tile)
    scale = jnp.exp(new_tile - peak)

    def join(i, state):
        total, parts = state
        tile = n.l_recv[i]
        scale = jnp.exp(tile - peak)
        part = n.a_recv[i].astype(F32)
        return (
            total + scale * pltpu.roll(tile, 64, 1),
            [acc + part[r * 8 : r * 8 + 8] * scale[:, r : r + 1] for r, acc in enumerate(parts)],
        )

    total, parts = lax.fori_loop(
        0,
        16,
        join,
        (
            scale * new_total,
            [new_out[r * 8 : r * 8 + 8] * scale[:, r : r + 1] for r in range(4)],
        ),
    )
    for r in range(4):
        n.q_rows[r * 8 : r * 8 + 8, :] = parts[r] / total[:, r : r + 1]
    for h, rows in enumerate((n.q_rot0, n.q_rot1)):
        for r in range(4):
            rows[pl.ds(r, 4, stride=4), :] = n.q_rows[r * 8 + h * 4 : r * 8 + h * 4 + 4, :]
    att = jnp.concatenate([n.q_rot0[...], n.q_rot1[...]], axis=1).astype(BF16)
    loads["wo"].wait()
    n.p_rows[...] = dot(att, n.v_wo[...])

    stage4_out(0)
    stage3_out(1)

    fd = n.v_down[...] - STEP_SCALE * summed(0)
    fd_out[...] = fd
    n.fd_pad[0:64, :] = jnp.zeros((64, 256), BF16)
    n.fd_pad[64:128, :] = fd.astype(BF16)
    low = dot(att, n.fd_pad[...], NT)

    o1 = rcopy(n.o_send1, n.o_recv1, n.s_o1_s.at[0], n.s_o1_r.at[0], sib)

    def out_part(part):
        for pair in range(4):
            both = []
            for e in (pair * 2, pair * 2 + 1):
                at = 160 * e // 128 * 128
                shift = 160 * e - at
                base = pl.multiple_of(part * 1280 + at, 128)
                window = n.p_rows[:, pl.ds(base, 256)]
                window = pltpu.roll(window, 256 - shift, 1) if shift else window
                both.append(
                    jnp.concatenate(
                        [window[:, :128], jnp.where(lane < 32, window[:, 128:], low)], axis=1
                    )
                )
            n.o_send1[part * 4 + pair] = jnp.where(c == 0, both[1], both[0]).astype(BF16)
            n.o_keep[part * 4 + pair] = jnp.where(c == 0, both[0], both[1])

    loop(4, out_part)
    o1.start()

    stage4_out(1)

    o1.wait_recv()

    def out_sum(i):
        n.o_send2[i] = (n.o_keep[i] + n.o_recv1[i].astype(F32)).astype(BF16)

    loop(16, out_sum)

    def o2(k):
        i = lax.rem(i0 + k, 16)
        return rcopy(
            n.o_send2.at[i], n.o_recv2.at[i0], n.s_o2_s.at[k], n.s_o2_r.at[i0], tdev(2 * i + c)
        )

    def o2_in(k):
        i = lax.rem(i0 + k, 16)
        return rcopy(
            n.o_send2.at[i], n.o_recv2.at[i], n.s_o2_s.at[k], n.s_o2_r.at[i], tdev(2 * i + c)
        )

    loop(16, lambda k: o2(k).start(), 1)

    first_col = 160 * t
    base = lax.div(first_col, 128) * 128
    up_cols = n.v_up[:, pl.ds(pl.multiple_of(base, 128), 256)]
    up_cols = pltpu.roll(up_cols, lax.rem(256 - (first_col - base), 256), 1)
    fu = up_cols - STEP_SCALE * summed(1)
    n.fu_pad[0:64, :] = jnp.zeros((64, 256), BF16)
    n.fu_pad[64:128, :] = fu.astype(BF16)

    owner = 4 * g + lax.div(t, 8)

    def f_copy(e):
        return rcopy(
            n.f_send.at[e], n.f_recv, n.s_f_s.at[e], n.s_f_r.at[0], tdev(8 * lax.rem(t, 4) + e)
        )

    @pl.when(lax.div(t, 4) == g)
    def _():
        n.fu_rows[...] = jnp.concatenate([fu, fu], axis=0).T
        for e in range(8):
            n.f_send[e] = n.fu_rows[20 * e : 20 * e + 24, :]
        for e in range(8):
            @pl.when(8 * lax.rem(t, 4) + e != t)
            def _():
                f_copy(e).start()

            @pl.when(8 * lax.rem(t, 4) + e == t)
            def _():
                n.f_recv[...] = n.f_send[e]

    loop(16, lambda k: o2_in(k).wait_recv(), 1)
    n.o_recv2[i0] = n.o_send2[i0]
    total = lax.fori_loop(
        1, 16, lambda i, a: a + n.o_recv2[i].astype(F32), n.o_recv2[0].astype(F32)
    )
    low = jnp.where(lane < 64, 0.0, total[:, 128:]).astype(BF16)
    decoded = total + adapter_scale * dot(low, n.fu_pad[...])
    wide_row = sublanes((16, 256))
    alive = (wide_row >> 2) < by_rollout(wide_row & 3, live)
    n.d_rows[...] = jnp.where(alive, decoded, 0.0)
    for s in range(4):
        dec_out[s] = n.d_rows[s * 4 : s * 4 + 4, 0:160].astype(BF16)

    @pl.when(owner != t)
    def _():
        f_copy(0).wait_recv()

    fu_out[...] = n.f_recv[0:20, 0:64]

    loop(8, lambda k: dn_z(k).wait_send(), 1)
    loop(8, lambda k: dn_y(k).wait_send())
    loop(16, lambda k: dn_c(k).wait_send())
    for copy in kv:
        copy.wait_send()
    loop(16, lambda k: q_copy(k).wait_send(), 1)
    loop(4, lambda k: n_copy(k).wait_send(), 1)

    def a_done(k):
        for copy in a_copy(k):
            copy.wait_send()

    loop(16, a_done, 1)

    @pl.when(c != y)
    def _():
        q_copy(0).wait_send()
        a_done(0)

    for u in range(2):
        loop(4, lambda k: g1(u, k).wait_send())
        loop(8, lambda k: g2(u, k).wait_send(), 1)
        loop(16, lambda k: g3(u, k).wait_send(), 1)
        loop(8, lambda k: g4(u, k).wait_send(), 1)
    o1.wait_send()
    loop(16, lambda k: o2(k).wait_send(), 1)

    @pl.when(lax.div(t, 4) == g)
    def _():
        for e in range(8):
            @pl.when(8 * lax.rem(t, 4) + e != t)
            def _():
                f_copy(e).wait_send()


def body(hid, cot, down, up, wo, wq, wk, wv, x, kc, vc, fill, start, live):
    hbm = pl.BlockSpec(memory_space=pl.ANY)
    smem = pl.BlockSpec(memory_space=pltpu.SMEM)
    vmem = pl.BlockSpec(memory_space=pltpu.VMEM)
    dec, fd, fu = pl.pallas_call(
        kernel,
        out_shape=(
            jax.ShapeDtypeStruct((4, 4, 160), BF16),
            jax.ShapeDtypeStruct((64, 256), F32),
            jax.ShapeDtypeStruct((20, 64), F32),
        ),
        in_specs=[hbm] * 11 + [smem] * 3,
        out_specs=(vmem,) * 3,
        scratch_shapes=[pltpu.VMEM(shape, kind) for shape, kind in SCRATCH.values()]
        + [pltpu.SemaphoreType.DMA(shape) for shape in SEMS.values()],
        compiler_params=pltpu.CompilerParams(
            collective_id=0, has_side_effects=True, vmem_limit_bytes=56 * 2**20
        ),
        name="update_and_decode",
    )(hid, cot, down.T, up, wo, wq, wk.T, wv.T, x, kc, vc, fill, start, live)
    return dec, fd.T, fu.T


def solution(mesh):
    return jax.shard_map(
        body,
        mesh=mesh,
        in_specs=(
            P(("group", "tensor"), None),
            P(("group", "tensor"), None),
            P("tensor", None),
            P(),
            P("tensor", None),
            P(None, "tensor"),
            P(None, "tensor"),
            P(None, "tensor"),
            P(None, "group", None),
            P("group", "tensor", None),
            P("group", "tensor", None),
            P("group"),
            P("group"),
            P("group"),
        ),
        out_specs=(P(None, "group", "tensor"), P("tensor", None), P(None, ("group", "tensor"))),
        check_vma=False,
    )
```

time: 654 us -> 73.5 us (0.11); the launches traced: 647 us -> 73.3 us
  waiting for transfers between devices: 352 us -> 0 us
  blocking collectives: 167 us -> 0 us
  other arithmetic: 78.7 us -> 0 us
  Pallas kernels: 0 us -> 68.5 us
  matrix products: 18.9 us -> 0 us
  between operations: 14.1 us -> 0.65 us
  local copies, waits for them, and re-layouts: 16 us -> 4.08 us
    all_gather x5 -> x0, blocking collectives: 167 us -> none  [the longest x2 64.1 us: joined(): gathered = jax.tree.map(lambda a: lax.all_gather(a, axis), part)]
    psum x1 -> x0, waiting for transfers between devices: 123 us -> none  [body(): lax.psum((down_gradient, up_gradient), ('group', 'tensor'))]
    all_gather x2 -> x0, waiting for transfers between devices: 117 us -> none  [the longest x1 98.7 us: joined(): gathered = jax.tree.map(lambda a: lax.all_gather(a, axis), part)]
    unnamed x5 -> x0, waiting for transfers between devices: 112 us -> none
    add x64 -> x0, other arithmetic: 70.5 us -> none  [the longest x31 48 us: join_parts(): first[2] * left[..., None] + second[2] * right[..., None]]
    pallas_call x0 -> x1, Pallas kernels: none -> 68.5 us  [body(): pl.pallas_call(kernel, out_shape=(jax.ShapeDtypeStruct((4, 4, 160), BF16)...]
    dot_general x10 -> x0, matrix products: 18.9 us -> none  [the longest x2 9.93 us: reduce_over_rows(): lax.dot_general(left, right, (((0,), (0,)), ((), ())), preferred_element_...]
  transfers between devices with their start and end apart: 4 -> 0, of which waited for: 4 -> 0; matrix products, arithmetic and copies ran while one was open for 4% -> 0% of each run, Pallas kernels for 0% -> 0%
where the time goes in v1:
time: 73.5 us; the launch traced here: 73.3 us
  Pallas kernels  68.5 us (93%)
  local copies, waits for them, and re-layouts  4.08 us (6%)
    pallas_call x1, Pallas kernels, body(): pl.pallas_call(kernel, out_shape=(jax.ShapeDtypeStruct((4, 4, 160), BF16)...  68.5 us
    unnamed x3, local copies, waits for them, and re-layouts  4.08 us

profile of v1, /device:TPU:3, one launch (start us, length us, event | category | flops | bytes accessed | tf_op | source)
XLA Modules:
  0.0 73.3 jit_solution(3261252231399635817)
XLA Ops:
  0.6 68.5 %update_and_decode.1 = (bf16[4,4,160]{2,1,0:T(4,128)(2,1)}, f32[64,256]{1,0:T(8,128)}, f32[20,64]{1,0:T(8,128)}) custom-call(bf16[128,8192]{1,0:T(8,128)(2,1)} %hid.1, bf16[128,5120]{1,0:T(8,128)(2,1)} %cot.1, f32[64,256]{1,0:T(8,128)} %bitcast.7, f32[64,5120]{1,0:T(8,128)} %up.1, bf16[256,5120]{1,0:T(8,128)(2,1)} %wo.1, bf16[5120,256]{1,0:T(8,128)(2,1)} %wq.1, ...), custom_call_target="tpu_custom_call" | custom-call | tf_op jit(solution)/shard_map/update_and_decode/pallas_call | solution.py:726
  69.2 1.3 %copy.20 = bf16[4,4,160]{2,1,0:T(4,128)(2,1)} copy(bf16[4,4,160]{2,1,0:T(4,128)(2,1)} %get-tuple-element.12) | data formatting | bytes 10240
  70.5 1.5 %copy.21 = f32[256,64]{0,1:T(8,128)} copy(f32[256,64]{0,1:T(8,128)} %bitcast.8) | data formatting | bytes 131072
  72.0 1.3 %copy.22 = f32[64,20]{0,1:T(8,128)} copy(f32[64,20]{0,1:T(8,128)} %bitcast.9) | data formatting | bytes 10240

commit v2 on v1

v2 whole, which is shorter than its diff:
```python
import math

import jax
import jax.numpy as jnp
from jax import lax
from jax.experimental import pallas as pl
from jax.experimental.pallas import tpu as pltpu
from jax.sharding import PartitionSpec as P

MESH = pl.DeviceIdType.MESH
F32 = jnp.float32
BF16 = jnp.bfloat16

adapter_scale = 0.01
rate_numerator = 50.0
rope_theta = 1000000.0
masked_score = -1e30

HD = 128
TOKENS = 32768
STEP_SCALE = adapter_scale * rate_numerator / math.sqrt(TOKENS)
INV_ROOT = 1.0 / math.sqrt(HD)

NN = (((1,), (0,)), ((), ()))
NT = (((1,), (1,)), ((), ()))


def dot(a, b, dims=NN):
    return lax.dot_general(a, b, dims, preferred_element_type=F32)


def rcopy(src, dst, ss, rs, dev):
    return pltpu.make_async_remote_copy(
        src_ref=src, dst_ref=dst, send_sem=ss, recv_sem=rs, device_id=dev, device_id_type=MESH
    )


def loop(n, fn, start=0):
    def step(k, carry):
        fn(k)
        return carry

    lax.fori_loop(start, n, step, 0)


SCRATCH = dict(
    v_down=((64, 256), F32),
    v_x=((4, 4, 5120), BF16),
    x_rows=((16, 5120), F32),
    v_wq=((5120, 256), BF16),
    v_wkv=((64, 5120), BF16),
    v_up=((64, 5120), F32),
    v_cot=((128, 5120), BF16),
    cot2=((128, 2560), BF16),
    hid2=((2, 128, 4096), BF16),
    v_wo=((256, 5120), BF16),
    kbuf=((2, 4, 128, 512), BF16),
    vbuf=((2, 4, 128, 512), BF16),
    down_own=((64, 256), BF16),
    down_half=((16, 64, 256), BF16),
    back2=((2, 64, 128), BF16),
    part_send=((64, 256), F32),
    part_recv=((64, 256), F32),
    q_rot0=((16, 128), F32),
    q_rot1=((16, 128), F32),
    q_rows=((32, 128), F32),
    q_send=((32, 128), BF16),
    q_buf=((16, 32, 128), BF16),
    n_buf=((4, 16, 128), BF16),
    n_send=((16, 128), BF16),
    a_send=((16, 32, 128), BF16),
    a_recv=((16, 32, 128), BF16),
    l_send=((16, 8, 128), F32),
    l_recv=((16, 8, 128), F32),
    d_send2=((8, 128, 256), BF16),
    d_recv2=((8, 128, 256), BF16),
    u_send2=((8, 160, 128), BF16),
    u_recv2=((8, 160, 128), BF16),
    g_send3=((2, 16, 16, 128), BF16),
    g_recv3=((2, 16, 16, 128), BF16),
    g_send4=((2, 16, 128), F32),
    g_recv4=((2, 8, 16, 128), F32),
    u_tmp=((64, 1280), F32),
    p_rows=((16, 5120), F32),
    fd_pad=((128, 256), BF16),
    fu_pad=((128, 256), BF16),
    o_send1=((16, 16, 256), BF16),
    o_keep=((16, 16, 256), F32),
    o_recv1=((16, 16, 256), BF16),
    o_send2=((16, 16, 256), BF16),
    o_recv2=((16, 16, 256), BF16),
    d_rows=((16, 256), F32),
    f_send=((8, 8, 128), F32),
    f_recv=((8, 8, 128), F32),
    w_dec=((4, 4, 160), BF16),
    w_fd=((64, 256), F32),
    w_fu=((20, 64), F32),
)
SEMS = dict(
    load=(11,),
    dn_sz=(1,),
    dn_sy=(1,),
    dn_r=(16,),
    sib_s=(4,),
    sib_r=(4,),
    bk=(2,),
    pt=(2,),
    q=(2,),
    n=(2,),
    a=(2,),
    l=(2,),
    g2=(2, 2),
    g3=(2, 2),
    g4=(2, 2),
    o1=(2,),
    o2=(2,),
    f=(2,),
    out=(3,),
)


class Names:
    pass


def lanes(shape):
    return lax.broadcasted_iota(jnp.int32, shape, len(shape) - 1)


def sublanes(shape):
    return lax.broadcasted_iota(jnp.int32, shape, len(shape) - 2)


def by_rollout(rollout, ref):
    picked = jnp.where(rollout == 0, ref[0], ref[1])
    picked = jnp.where(rollout == 2, ref[2], picked)
    return jnp.where(rollout == 3, ref[3], picked)


def kernel(
    hid, cot, down, up, wo, wq, wk, wv, x, kc, vc, fill, start, live, dec_out, fd_out, fu_out, *refs
):
    n = Names()
    for name, ref in zip(list(SCRATCH) + ["s_" + key for key in SEMS], refs):
        setattr(n, name, ref)
    t = lax.axis_index("tensor")
    g = lax.axis_index("group")
    c = lax.rem(t, 2)
    i0 = lax.div(t, 2)
    y = lax.div(t, 16)
    z = lax.rem(i0, 8)
    t16 = lax.rem(t, 16)
    sib = {"tensor": t + 1 - 2 * c}
    other_y = lax.rem(t + 16, 32)
    g_other = g + 1 - 2 * lax.rem(g, 2)
    relays = c == y

    def tdev(index):
        return {"tensor": index}

    def gdev(index):
        return {"group": index}

    def near(k):
        return lax.rem(lax.div(k + 1, 2) * (7 - 6 * lax.rem(k, 2)), 8)

    f_from = 4 * g + lax.div(t, 8)
    f_self = f_from == t

    def f_to(e):
        return {"group": lax.div(t, 4), "tensor": 8 * lax.rem(t, 4) + e}

    def arrived(buf, count, sem):
        part = buf.at[pl.ds(0, count)]
        rcopy(part, part, sem, sem, sib).wait_recv()

    def left(buf, count, sem):
        part = buf.at[pl.ds(0, count)]
        rcopy(part, part, sem, sem, sib).wait_send()

    def arrived_heads(buf, sem):
        @pl.when(relays)
        def _():
            arrived(buf, 15, sem)

        @pl.when(jnp.logical_not(relays))
        def _():
            arrived(buf, 16, sem)

    barrier = pltpu.get_barrier_semaphore()
    loop(
        32,
        lambda k: pl.semaphore_signal(
            barrier, inc=1, device_id=tdev(lax.rem(t + k, 32)), device_id_type=MESH
        ),
        1,
    )
    loop(
        8,
        lambda k: pl.semaphore_signal(
            barrier, inc=1, device_id=gdev(lax.rem(g + k, 8)), device_id_type=MESH
        ),
        1,
    )

    pl.semaphore_signal(
        barrier,
        inc=1,
        device_id={"group": g_other, "tensor": other_y},
        device_id_type=MESH,
    )

    def f_greet(j):
        pl.semaphore_signal(
            barrier, inc=1, device_id={"group": j, "tensor": f_from}, device_id_type=MESH
        )

    loop(8, lambda k: f_greet(lax.rem(g + k, 8)), 1)

    @pl.when(jnp.logical_not(f_self))
    def _():
        f_greet(g)

    def half(size, which):
        return pl.ds(pl.multiple_of(size * which, size), size)

    loads = dict(
        down=(down, n.v_down),
        x=(x, n.v_x),
        wq=(wq, n.v_wq),
        wk=(wk, n.v_wkv.at[pl.ds(0, 32)]),
        wv=(wv, n.v_wkv.at[pl.ds(32, 32)]),
        up=(up, n.v_up),
        cot=(cot, n.v_cot),
        hid=(hid.at[:, half(4096, c)], n.hid2.at[0]),
        k=(kc.at[:, :, half(512, c)], n.kbuf.at[0]),
        v=(vc.at[:, :, half(512, c)], n.vbuf.at[0]),
        wo=(wo, n.v_wo),
    )
    loads = {
        key: pltpu.make_async_copy(src, dst, n.s_load.at[at])
        for at, (key, (src, dst)) in enumerate(loads.items())
    }
    for copy in loads.values():
        copy.start()

    loads["down"].wait()
    n.down_own[...] = n.v_down[...].astype(BF16)

    pl.semaphore_wait(barrier, 47 - f_self.astype(jnp.int32))

    def dn_z(k):
        to = y * 16 + lax.rem(z + near(k), 8) * 2 + y
        return rcopy(
            n.down_own, n.down_half.at[t16], n.s_dn_sz.at[0], n.s_dn_r.at[t16], tdev(to)
        )

    def dn_y(slot, group):
        return rcopy(
            n.down_half.at[slot],
            n.down_half.at[slot],
            n.s_dn_sy.at[0],
            n.s_dn_r.at[slot],
            {"group": group, "tensor": other_y},
        )

    def dn_pass(z_of, core):
        dn_y(z_of * 2 + core, g + core * (g_other - g)).start()

    loop(8, lambda k: dn_z(k).start(), 1)

    @pl.when(relays)
    def _():
        n.down_half[t16] = n.down_own[...]
        dn_pass(z, c)

    @pl.when(jnp.logical_not(relays))
    def _():
        dn_z(0).start()

    pairs = [
        rcopy(src, dst, n.s_sib_s.at[at], n.s_sib_r.at[at], sib)
        for at, (src, dst) in enumerate(
            (
                (hid.at[:, half(4096, 1 - c)], n.hid2.at[1]),
                (kc.at[:, :, half(512, 1 - c)], n.kbuf.at[1]),
                (vc.at[:, :, half(512, 1 - c)], n.vbuf.at[1]),
                (cot.at[:, half(2560, 1 - c)], n.cot2),
            )
        )
    ]
    for copy in pairs:
        copy.start()

    loads["x"].wait()
    for s in range(4):
        n.x_rows[s * 4 : s * 4 + 4, :] = n.v_x[s].astype(F32)
    xb = n.x_rows[...].astype(BF16)
    row = sublanes((16, HD))
    lane = lanes((16, HD))
    position = (by_rollout(row & 3, start) + (row >> 2)).astype(F32)
    freq = jnp.exp((lane & 63).astype(F32) * (-math.log(rope_theta) * 2.0 / HD))
    angle = position * freq
    cosine = jnp.cos(angle)
    sine = jnp.where(lane < 64, -jnp.sin(angle), jnp.sin(angle))

    def rotate(v):
        v = v.astype(BF16).astype(F32)
        return v * cosine + pltpu.roll(v, 64, 1) * sine

    loads["wq"].wait()
    q = dot(xb, n.v_wq[...])
    for h, rows in enumerate((n.q_rot0, n.q_rot1)):
        rows[...] = rotate(q[:, h * HD : (h + 1) * HD])
        for r in range(4):
            n.q_rows[r * 8 + h * 4 : r * 8 + h * 4 + 4, :] = rows[pl.ds(r, 4, stride=4), :]
    n.q_send[...] = n.q_rows[...].astype(BF16)

    def q_copy(k):
        i = lax.rem(i0 + k, 16)
        return rcopy(n.q_send, n.q_buf.at[t16], n.s_q.at[0], n.s_q.at[1], tdev(2 * i + y))

    @pl.when(jnp.logical_not(relays))
    def _():
        q_copy(0).start()

    loop(16, lambda k: q_copy(k).start(), 1)

    @pl.when(relays)
    def _():
        n.q_buf[t16] = n.q_send[...]

    send2 = (n.d_send2, n.u_send2)
    recv2 = (n.d_recv2, n.u_recv2)

    def g2(u, k):
        j = lax.rem(g + k, 8)
        return rcopy(
            send2[u].at[j], recv2[u].at[g], n.s_g2.at[u, 0], n.s_g2.at[u, 1], gdev(j)
        )

    def g3(u, k):
        i = lax.rem(t16 + k, 16)
        return rcopy(
            n.g_send3.at[u, i], n.g_recv3.at[u, i0], n.s_g3.at[u, 0], n.s_g3.at[u, 1],
            tdev(16 * c + i),
        )

    def g4(u, k):
        j = lax.rem(g + k, 8)
        return rcopy(
            n.g_send4.at[u], n.g_recv4.at[u, g], n.s_g4.at[u, 0], n.s_g4.at[u, 1], gdev(j)
        )

    def stack8(first, second, j):
        rows = slice(j * 8, j * 8 + 8)
        return jnp.concatenate([first[rows], second[rows]], axis=0).astype(BF16)

    def stage3_out(u):
        arrived(recv2[u], 7, n.s_g2.at[u, 1])
        recv2[u][g] = send2[u][g]

        def total(row):
            rows = pl.ds(pl.multiple_of(row, 16), 16)
            sums = recv2[u][0, rows, :].astype(F32)
            for j in range(1, 8):
                sums = sums + recv2[u][j, rows, :].astype(F32)
            return sums

        def send(i, low, high):
            n.g_send3[u, i] = jnp.concatenate([low, high], axis=0).astype(BF16)

        def down_sum(pair):
            sums = total(pair * 16)
            for e in range(2):
                piece = sums[e * 8 : e * 8 + 8]
                send(pair * 2 + e, piece[:, :128], piece[:, 128:])

        def up_sum(part):
            rest = total(128 + part * 16)
            for pair in range(4):
                sums = total(part * 64 + pair * 16)
                high = pltpu.roll(rest, 128 - 32 * pair, 1) if pair else rest
                for e in range(2):
                    rows = slice(e * 8, e * 8 + 8)
                    send(part * 8 + pair * 2 + e, sums[rows], high[rows])

        if u == 0:
            loop(8, down_sum)
        else:
            loop(2, up_sum)

        @pl.when(jnp.logical_not(relays))
        def _():
            g3(u, 0).start()

        loop(16, lambda k: g3(u, k).start(), 1)

    def stage4_out(u):
        arrived_heads(n.g_recv3.at[u], n.s_g3.at[u, 1])

        @pl.when(relays)
        def _():
            n.g_recv3[u, i0] = n.g_send3[u, t16]

        total = n.g_recv3[u, 0].astype(F32)
        for i in range(1, 16):
            total = total + n.g_recv3[u, i].astype(F32)
        n.g_send4[u] = total
        n.g_recv4[u, g] = total
        loop(8, lambda k: g4(u, k).start(), 1)
        return total

    def summed(u):
        arrived(n.g_recv4.at[u], 7, n.s_g4.at[u, 1])
        pieces = [n.g_recv4[u, j] for j in range(8)]
        return jnp.concatenate(
            [jnp.concatenate([p[:8], p[8:]], axis=1) for p in pieces], axis=0
        )

    loads["up"].wait()
    loads["cot"].wait()
    n.back2[0] = dot(n.v_up[...].astype(BF16), n.v_cot[...], NT).astype(BF16)
    bk = rcopy(n.back2.at[0], n.back2.at[1], n.s_bk.at[0], n.s_bk.at[1], sib)
    bk.start()

    loads["wk"].wait()
    loads["wv"].wait()
    nkv = dot(xb, n.v_wkv[...], NT)
    n.n_send[...] = jnp.concatenate([nkv, nkv], axis=1).astype(BF16)
    b4 = lax.rem(t, 4)

    def n_copy(k):
        to = t - b4 + lax.rem(b4 + k, 4)
        return rcopy(n.n_send, n.n_buf.at[b4], n.s_n.at[0], n.s_n.at[1], tdev(to))

    loop(4, lambda k: n_copy(k).start(), 1)
    n.n_buf[b4] = n.n_send[...]

    loads["hid"].wait()
    pairs[0].wait_recv()
    bk.wait_recv()

    back = jnp.concatenate([n.back2[0], n.back2[1]], axis=1)

    def down_pair(pair):
        blocks = []
        for e in range(2):
            cols = pl.ds(pl.multiple_of((pair * 2 + e) * 256, 256), 256)
            both = jnp.concatenate([n.hid2[0, :, cols], n.hid2[1, :, cols]], axis=0)
            blocks.append(dot(back, both))
        rows = pl.ds(pl.multiple_of(pair * 16, 16), 16)
        for j in range(8):
            n.d_send2[j, rows, :] = stack8(*blocks, j)

    loop(8, down_pair)
    loop(8, lambda k: g2(0, k).start(), 1)

    def dn_recv(slot):
        dn_y(slot, g).wait_recv()

    @pl.when(relays)
    def _():
        dn_recv(z * 2 + 1 - c)
        dn_pass(z, 1 - c)

        def pass_on(k):
            from_z = lax.rem(z + near(k), 8)
            for core in range(2):
                dn_recv(from_z * 2 + core)
                dn_pass(from_z, core)

        loop(8, pass_on, 1)

    arrived_heads(n.q_buf, n.s_q.at[1])
    loads["k"].wait()
    loads["v"].wait()
    pairs[1].wait_recv()
    pairs[2].wait_recv()

    spot = lanes((32, 256))
    spot = jnp.where(spot < 128, t * 128 + spot, (t + 1 - 2 * c) * 128 + spot - 128)
    tile_lane = lanes((8, 128))

    def attend(kk):
        cols = pl.ds(pl.multiple_of(kk * HD, HD), HD)
        qs = [n.q_buf[kk * 4 + j].astype(F32) for j in range(4)]
        outs, tops, sums = [], [], []
        for r in range(4):
            qr = jnp.concatenate([a[r * 8 : r * 8 + 8] for a in qs], axis=0).astype(BF16)
            keys = jnp.concatenate([n.kbuf[0, r, :, cols], n.kbuf[1, r, :, cols]], axis=0)
            values = jnp.concatenate([n.vbuf[0, r, :, cols], n.vbuf[1, r, :, cols]], axis=0)
            valid = spot < fill[r]
            scores = jnp.where(valid, dot(qr, keys, NT) * INV_ROOT, masked_score)
            top = jnp.max(scores, axis=1, keepdims=True)
            weights = jnp.where(valid, jnp.exp(scores - top), 0.0)
            tops.append(top)
            sums.append(jnp.sum(weights, axis=1, keepdims=True))
            outs.append(dot(weights.astype(BF16), values))
        for j in range(4):
            rows = slice(j * 8, j * 8 + 8)
            n.a_send[kk * 4 + j] = jnp.concatenate([o[rows] for o in outs], axis=0).astype(BF16)
            tile = jnp.zeros((8, 128), F32)
            for r in range(4):
                tile = jnp.where(tile_lane == r, tops[r][rows], tile)
                tile = jnp.where(tile_lane == 64 + r, sums[r][rows], tile)
            n.l_send[kk * 4 + j] = tile

    loop(2, attend)

    @pl.when(jnp.logical_not(relays))
    def _():
        loop(16, dn_recv)

    def reduce_part(part, total):
        for e in range(4):
            at = part * 4 + e
            cols = pl.ds(pl.multiple_of(at * 256, 256), 256)
            both = jnp.concatenate([n.hid2[0, :, cols], n.hid2[1, :, cols]], axis=0)
            total = total + dot(n.down_half[at], both, NT)
        return total

    n.part_send[...] = lax.fori_loop(0, 4, reduce_part, jnp.zeros((64, 256), F32))
    pt = rcopy(n.part_send, n.part_recv, n.s_pt.at[0], n.s_pt.at[1], sib)
    pt.start()

    stage3_out(0)
    loop(4, attend, 2)

    def a_copy(k):
        i = lax.rem(t16 + k, 16)
        to = tdev(16 * c + i)
        return (
            rcopy(n.a_send.at[i], n.a_recv.at[i0], n.s_a.at[0], n.s_a.at[1], to),
            rcopy(n.l_send.at[i], n.l_recv.at[i0], n.s_l.at[0], n.s_l.at[1], to),
        )

    def a_start(k):
        for copy in a_copy(k):
            copy.start()

    @pl.when(jnp.logical_not(relays))
    def _():
        a_start(0)

    loop(16, a_start, 1)

    @pl.when(relays)
    def _():
        n.a_recv[i0] = n.a_send[t16]
        n.l_recv[i0] = n.l_send[t16]

    pt.wait_recv()
    pairs[3].wait_recv()
    reduced = jnp.concatenate(
        [
            n.part_send[:, :128] + n.part_recv[:, 128:],
            n.part_send[:, 128:] + n.part_recv[:, :128],
        ],
        axis=1,
    ).astype(BF16)

    def up_part(part):
        both = jnp.concatenate(
            [
                n.v_cot[:, pl.ds(pl.multiple_of(2560 * c + 1280 * part, 1280), 1280)],
                n.cot2[:, pl.ds(pl.multiple_of(1280 * part, 1280), 1280)],
            ],
            axis=0,
        )
        n.u_tmp[...] = dot(reduced, both)
        rest = [jnp.zeros((64, 128), F32)] * 2
        quarter = lanes((64, 128)) >> 5
        for pair in range(4):
            low = []
            for e in range(2):
                first = 160 * (pair * 2 + e)
                at = first // 128 * 128
                window = n.u_tmp[:, at : at + 256]
                window = pltpu.roll(window, 256 - (first - at), 1) if first > at else window
                low.append(window[:, :128])
                high = pltpu.roll(window[:, 128:], 32 * pair, 1) if pair else window[:, 128:]
                rest[e] = jnp.where(quarter == pair, high, rest[e])
            rows = pl.ds(pl.multiple_of(part * 64 + pair * 16, 16), 16)
            for j in range(8):
                n.u_send2[j, rows, :] = stack8(*low, j)
        rows = pl.ds(pl.multiple_of(128 + part * 16, 16), 16)
        for j in range(8):
            n.u_send2[j, rows, :] = stack8(*rest, j)

    loop(2, up_part)
    loop(8, lambda k: g2(1, k).start(), 1)

    arrived(n.n_buf, 3, n.s_n.at[1])
    fresh = [n.n_buf[j].astype(F32) for j in range(4)]
    quarter = lane >> 5
    new_k = fresh[0]
    new_v = pltpu.roll(fresh[0], 96, 1)
    for j in range(1, 4):
        new_k = jnp.where(quarter == j, pltpu.roll(fresh[j], 32 * j, 1), new_k)
        new_v = jnp.where(quarter == j, pltpu.roll(fresh[j], (32 * j + 96) % 128, 1), new_v)
    new_k = rotate(new_k).astype(BF16)
    new_v = new_v.astype(BF16)
    nrow = sublanes((32, 16))
    ncol = lanes((32, 16))
    new_valid = ((nrow >> 3) == (ncol & 3)) & ((ncol >> 2) <= (nrow & 3))
    new_scores = jnp.where(new_valid, dot(n.q_send[...], new_k, NT) * INV_ROOT, masked_score)
    new_top = jnp.max(new_scores, axis=1, keepdims=True)
    new_weights = jnp.where(new_valid, jnp.exp(new_scores - new_top), 0.0)
    new_sum = jnp.sum(new_weights, axis=1, keepdims=True)
    new_out = dot(new_weights.astype(BF16), new_v)
    new_tile = jnp.zeros((8, 128), F32)
    new_total = jnp.zeros((8, 128), F32)
    for r in range(4):
        rows = slice(r * 8, r * 8 + 8)
        new_tile = jnp.where(tile_lane == r, new_top[rows], new_tile)
        new_total = jnp.where(tile_lane == r, new_sum[rows], new_total)

    stage4_out(0)
    arrived_heads(n.a_recv, n.s_a.at[1])
    arrived_heads(n.l_recv, n.s_l.at[1])

    stage3_out(1)

    peak = lax.fori_loop(0, 16, lambda i, m: jnp.maximum(m, n.l_recv[i]), new_tile)
    scale = jnp.exp(new_tile - peak)

    def join(i, state):
        total, parts = state
        tile = n.l_recv[i]
        scale = jnp.exp(tile - peak)
        part = n.a_recv[i].astype(F32)
        return (
            total + scale * pltpu.roll(tile, 64, 1),
            [acc + part[r * 8 : r * 8 + 8] * scale[:, r : r + 1] for r, acc in enumerate(parts)],
        )

    total, parts = lax.fori_loop(
        0,
        16,
        join,
        (
            scale * new_total,
            [new_out[r * 8 : r * 8 + 8] * scale[:, r : r + 1] for r in range(4)],
        ),
    )
    for r in range(4):
        n.q_rows[r * 8 : r * 8 + 8, :] = parts[r] / total[:, r : r + 1]
    for h, rows in enumerate((n.q_rot0, n.q_rot1)):
        for r in range(4):
            rows[pl.ds(r, 4, stride=4), :] = n.q_rows[r * 8 + h * 4 : r * 8 + h * 4 + 4, :]
    att = jnp.concatenate([n.q_rot0[...], n.q_rot1[...]], axis=1).astype(BF16)
    loads["wo"].wait()
    n.p_rows[...] = dot(att, n.v_wo[...])

    fd = n.v_down[...] - STEP_SCALE * summed(0)
    n.w_fd[...] = fd
    results = [
        pltpu.make_async_copy(src, dst, n.s_out.at[at])
        for at, (src, dst) in enumerate(
            ((n.w_dec, dec_out), (n.w_fd, fd_out), (n.w_fu, fu_out))
        )
    ]
    results[1].start()
    n.fd_pad[0:64, :] = jnp.zeros((64, 256), BF16)
    n.fd_pad[64:128, :] = fd.astype(BF16)
    low = dot(att, n.fd_pad[...], NT)

    o1 = rcopy(n.o_send1, n.o_recv1, n.s_o1.at[0], n.s_o1.at[1], sib)

    def out_part(part):
        for pair in range(4):
            both = []
            for e in (pair * 2, pair * 2 + 1):
                at = 160 * e // 128 * 128
                shift = 160 * e - at
                base = pl.multiple_of(part * 1280 + at, 128)
                window = n.p_rows[:, pl.ds(base, 256)]
                window = pltpu.roll(window, 256 - shift, 1) if shift else window
                both.append(
                    jnp.concatenate(
                        [window[:, :128], jnp.where(lane < 32, window[:, 128:], low)], axis=1
                    )
                )
            n.o_send1[part * 4 + pair] = jnp.where(c == 0, both[1], both[0]).astype(BF16)
            n.o_keep[part * 4 + pair] = jnp.where(c == 0, both[0], both[1])

    loop(4, out_part)
    o1.start()

    o1.wait_recv()

    def out_sum(i):
        n.o_send2[i] = (n.o_keep[i] + n.o_recv1[i].astype(F32)).astype(BF16)

    loop(16, out_sum)

    def o2(k):
        i = lax.rem(i0 + k, 16)
        return rcopy(
            n.o_send2.at[i], n.o_recv2.at[i0], n.s_o2.at[0], n.s_o2.at[1], tdev(2 * i + c)
        )

    loop(16, lambda k: o2(k).start(), 1)

    up_total = stage4_out(1)
    up_total = jnp.concatenate([up_total[:8], up_total[8:]], axis=1)
    for e in range(8):
        n.f_send[e] = pltpu.roll(up_total, (256 - 20 * e) % 256, 1)[:, :128]

    def f_copy(e):
        return rcopy(n.f_send.at[e], n.f_recv.at[g], n.s_f.at[0], n.s_f.at[1], f_to(e))

    f_own = lax.rem(t, 8)

    def f_start(e):
        @pl.when(jnp.logical_not(f_self & (e == f_own)))
        def _():
            f_copy(e).start()

    loop(8, f_start)

    @pl.when(f_self)
    def _():
        n.f_recv[g] = n.f_send[f_own]

    def left_heads(buf, sem):
        @pl.when(relays)
        def _():
            left(buf, 15, sem)

        @pl.when(jnp.logical_not(relays))
        def _():
            left(buf, 16, sem)

    @pl.when(relays)
    def _():
        left(n.down_half, 7, n.s_dn_sz.at[0])
        left(n.down_half, 16, n.s_dn_sy.at[0])

    @pl.when(jnp.logical_not(relays))
    def _():
        left(n.down_half, 8, n.s_dn_sz.at[0])

    left_heads(n.q_buf, n.s_q.at[0])
    left(n.n_buf, 3, n.s_n.at[0])
    for copy in pairs:
        copy.wait_send()
    bk.wait_send()
    pt.wait_send()
    left_heads(n.a_send, n.s_a.at[0])
    left_heads(n.l_send, n.s_l.at[0])
    left(n.d_send2, 7, n.s_g2.at[0, 0])
    left(n.u_send2, 7, n.s_g2.at[1, 0])
    left_heads(n.g_send3.at[0], n.s_g3.at[0, 0])
    left(n.g_recv4.at[0], 7, n.s_g4.at[0, 0])

    first_col = 160 * t
    base = lax.div(first_col, 128) * 128
    up_cols = n.v_up[:, pl.ds(pl.multiple_of(base, 128), 256)]
    up_cols = pltpu.roll(up_cols, lax.rem(256 - (first_col - base), 256), 1)
    fu = up_cols - STEP_SCALE * summed(1)
    n.fu_pad[0:64, :] = jnp.zeros((64, 256), BF16)
    n.fu_pad[64:128, :] = fu.astype(BF16)

    arrived(n.o_recv2, 15, n.s_o2.at[1])
    n.o_recv2[i0] = n.o_send2[i0]
    total = lax.fori_loop(
        1, 16, lambda i, a: a + n.o_recv2[i].astype(F32), n.o_recv2[0].astype(F32)
    )
    low = jnp.where(lane < 64, 0.0, total[:, 128:]).astype(BF16)
    decoded = total + adapter_scale * dot(low, n.fu_pad[...])
    wide_row = sublanes((16, 256))
    alive = (wide_row >> 2) < by_rollout(wide_row & 3, live)
    n.d_rows[...] = jnp.where(alive, decoded, 0.0)
    for s in range(4):
        n.w_dec[s] = n.d_rows[s * 4 : s * 4 + 4, 0:160].astype(BF16)
    results[0].start()

    @pl.when(f_self)
    def _():
        arrived(n.f_recv, 7, n.s_f.at[1])

    @pl.when(jnp.logical_not(f_self))
    def _():
        arrived(n.f_recv, 8, n.s_f.at[1])

    first_col = 640 * g + 20 * t
    base = jnp.minimum(lax.div(first_col, 128) * 128, 5120 - 256)
    up_cols = n.v_up[:, pl.ds(pl.multiple_of(base, 128), 256)]
    up_cols = pltpu.roll(up_cols, lax.rem(256 - (first_col - base), 256), 1)[:, :128]
    sums = jnp.concatenate([n.f_recv[j] for j in range(8)], axis=0)
    piece = up_cols - STEP_SCALE * sums
    n.w_fu[...] = jnp.concatenate([piece, piece], axis=0).T[0:20, 0:64]
    results[2].start()

    left_heads(n.g_send3.at[1], n.s_g3.at[1, 0])
    left(n.g_recv4.at[1], 7, n.s_g4.at[1, 0])
    o1.wait_send()
    left(n.o_send2, 15, n.s_o2.at[0])

    @pl.when(f_self)
    def _():
        left(n.f_send, 7, n.s_f.at[0])

    @pl.when(jnp.logical_not(f_self))
    def _():
        left(n.f_send, 8, n.s_f.at[0])

    for copy in results:
        copy.wait()


def hand_out(dec, fd, fu, dec_out, fd_out, fu_out):
    dec_out[...] = dec[...]
    fd_out[...] = fd[...]
    fu_out[...] = fu[...]


def body(hid, cot, down, up, wo, wq, wk, wv, x, kc, vc, fill, start, live):
    hbm = pl.BlockSpec(memory_space=pl.ANY)
    smem = pl.BlockSpec(memory_space=pltpu.SMEM)
    vmem = pl.BlockSpec(memory_space=pltpu.VMEM)
    shapes = (
        jax.ShapeDtypeStruct((4, 4, 160), BF16),
        jax.ShapeDtypeStruct((64, 256), F32),
        jax.ShapeDtypeStruct((20, 64), F32),
    )
    results = pl.pallas_call(
        kernel,
        out_shape=shapes,
        in_specs=[hbm] * 11 + [smem] * 3,
        out_specs=(hbm,) * 3,
        scratch_shapes=[pltpu.VMEM(shape, kind) for shape, kind in SCRATCH.values()]
        + [pltpu.SemaphoreType.DMA(shape) for shape in SEMS.values()],
        compiler_params=pltpu.CompilerParams(
            collective_id=0, has_side_effects=True, vmem_limit_bytes=56 * 2**20
        ),
        name="update_and_decode",
    )(hid, cot, down.T, up, wo, wq, wk.T, wv.T, x, kc, vc, fill, start, live)
    dec, fd, fu = pl.pallas_call(
        hand_out,
        out_shape=shapes,
        in_specs=[vmem] * 3,
        out_specs=(vmem,) * 3,
        compiler_params=pltpu.CompilerParams(vmem_limit_bytes=56 * 2**20),
        name="hand_out",
    )(*results)
    return dec, fd.T, fu.T


def solution(mesh):
    return jax.shard_map(
        body,
        mesh=mesh,
        in_specs=(
            P(("group", "tensor"), None),
            P(("group", "tensor"), None),
            P("tensor", None),
            P(),
            P("tensor", None),
            P(None, "tensor"),
            P(None, "tensor"),
            P(None, "tensor"),
            P(None, "group", None),
            P("group", "tensor", None),
            P("group", "tensor", None),
            P("group"),
            P("group"),
            P("group"),
        ),
        out_specs=(P(None, "group", "tensor"), P("tensor", None), P(None, ("group", "tensor"))),
        check_vma=False,
    )
```

time: 73.5 us -> 55.8 us (0.76)
  Pallas kernels: 68.5 us -> 55.1 us
  local copies, waits for them, and re-layouts: 4.08 us -> 0 us
    pallas_call x1 -> x2, Pallas kernels: 68.5 us -> 55.1 us  [the longest x1 53.6 us: body(): pl.pallas_call(kernel, out_shape=shapes, in_specs=[hbm] * 11 + [smem] * 3...]
    unnamed x3 -> x0, local copies, waits for them, and re-layouts: 4.08 us -> none
where the time goes in v2:
time: 55.8 us; the launch traced here: 55.7 us
  Pallas kernels  55.1 us (99%)
  between operations  0.64 us (1%)
    pallas_call x1, Pallas kernels, body(): pl.pallas_call(kernel, out_shape=shapes, in_specs=[hbm] * 11 + [smem] * 3...  53.6 us
    pallas_call x1, Pallas kernels, body(): pl.pallas_call(hand_out, out_shape=shapes, in_specs=[vmem] * 3, out_specs...  1.48 us

profile of v2, /device:TPU:3, one launch (start us, length us, event | category | flops | bytes accessed | tf_op | source)
XLA Modules:
  0.0 55.7 jit_solution(8673313338832078187)
XLA Ops:
  0.6 53.6 %update_and_decode.1 = (bf16[4,4,160]{2,1,0:T(4,128)(2,1)}, f32[64,256]{1,0:T(8,128)}, f32[20,64]{1,0:T(8,128)}) custom-call(bf16[128,8192]{1,0:T(8,128)(2,1)} %hid.1, bf16[128,5120]{1,0:T(8,128)(2,1)} %cot.1, f32[64,256]{1,0:T(8,128)} %bitcast.7, f32[64,5120]{1,0:T(8,128)} %up.1, bf16[256,5120]{1,0:T(8,128)(2,1)} %wo.1, bf16[5120,256]{1,0:T(8,128)(2,1)} %wq.1, ...), custom_call_target="tpu_custom_call" | custom-call | tf_op jit(solution)/shard_map/update_and_decode/pallas_call | solution.py:829
  54.2 1.5 %hand_out.1 = (bf16[4,4,160]{2,1,0:T(4,128)(2,1)}, f32[64,256]{1,0:T(8,128)}, f32[20,64]{1,0:T(8,128)}) custom-call(bf16[4,4,160]{2,1,0:T(4,128)(2,1)} %get-tuple-element.9.dec, f32[64,256]{1,0:T(8,128)} %get-tuple-element.10.fd, f32[20,64]{1,0:T(8,128)} %get-tuple-element.11.fu), custom_call_target="tpu_custom_call" | custom-call | tf_op jit(solution)/shard_map/hand_out/pallas_call | solution.py:841

commit v3 on v2

--- a/solution.py
+++ b/solution.py
@@ -73,11 +73,11 @@
     l_send=((16, 8, 128), F32),
     l_recv=((16, 8, 128), F32),
     d_send2=((8, 128, 256), BF16),
-    d_recv2=((8, 128, 256), BF16),
+    d_recv2=((4, 2, 128, 256), BF16),
     u_send2=((8, 160, 128), BF16),
-    u_recv2=((8, 160, 128), BF16),
-    g_send3=((2, 16, 16, 128), BF16),
-    g_recv3=((2, 16, 16, 128), BF16),
+    u_recv2=((4, 2, 160, 128), BF16),
+    g_send3=((2, 32, 16, 128), BF16),
+    g_recv3=((2, 32, 16, 128), BF16),
     g_send4=((2, 16, 128), F32),
     g_recv4=((2, 8, 16, 128), F32),
     u_tmp=((64, 1280), F32),
@@ -97,7 +97,7 @@
     w_fu=((20, 64), F32),
 )
 SEMS = dict(
-    load=(11,),
+    load=(14,),
     dn_sz=(1,),
     dn_sy=(1,),
     dn_r=(16,),
@@ -138,10 +138,10 @@
 
 
 def kernel(
-    hid, cot, down, up, wo, wq, wk, wv, x, kc, vc, fill, start, live, dec_out, fd_out, fu_out, *refs
+    hid, cot, down, up, wo, wq, wk, wv, x, kc, vc, fill_in, start_in, live_in, dec_out, fd_out, fu_out, *refs
 ):
     n = Names()
-    for name, ref in zip(list(SCRATCH) + ["s_" + key for key in SEMS], refs):
+    for name, ref in zip(list(SCRATCH) + ["start", "fill", "live"] + ["s_" + key for key in SEMS], refs):
         setattr(n, name, ref)
     t = lax.axis_index("tensor")
     g = lax.axis_index("group")
@@ -153,6 +153,8 @@
     sib = {"tensor": t + 1 - 2 * c}
     other_y = lax.rem(t + 16, 32)
     g_other = g + 1 - 2 * lax.rem(g, 2)
+    gx = lax.div(g, 2)
+    gy = lax.rem(g, 2)
     relays = c == y
 
     def tdev(index):
@@ -164,11 +166,53 @@
     def near(k):
         return lax.rem(lax.div(k + 1, 2) * (7 - 6 * lax.rem(k, 2)), 8)
 
+    def far_z(k):
+        return lax.rem(z + near(7 - k), 8)
+
+    def far_core(k):
+        return far_z(lax.div(k, 2)) * 2 + lax.rem(c + 1 + k, 2)
+
+    def far_chip(k):
+        return lax.rem(y + 1 + k, 2) * 8 + far_z(lax.div(k, 2))
+
+    def far_x(k):
+        at = 3 - k
+        return lax.rem(gx + lax.div(at + 1, 2) * (3 - 2 * lax.rem(at, 2)), 4)
+
+    def far_group(k):
+        return far_x(lax.rem(k, 4)) * 2 + lax.rem(g + 1 - lax.div(k, 4), 2)
+
     f_from = 4 * g + lax.div(t, 8)
     f_self = f_from == t
 
     def f_to(e):
         return {"group": lax.div(t, 4), "tensor": 8 * lax.rem(t, 4) + e}
+
+    def half(size, which):
+        return pl.ds(pl.multiple_of(size * which, size), size)
+
+    loads = dict(
+        down=(down, n.v_down),
+        x=(x, n.v_x),
+        wq=(wq, n.v_wq),
+        wk=(wk, n.v_wkv.at[pl.ds(0, 32)]),
+        wv=(wv, n.v_wkv.at[pl.ds(32, 32)]),
+        up=(up, n.v_up),
+        cot=(cot, n.v_cot),
+        hid=(hid.at[:, half(4096, c)], n.hid2.at[0]),
+        k=(kc.at[:, :, half(512, c)], n.kbuf.at[0]),
+        v=(vc.at[:, :, half(512, c)], n.vbuf.at[0]),
+        wo=(wo, n.v_wo),
+        start=(start_in, n.start),
+        fill=(fill_in, n.fill),
+        live=(live_in, n.live),
+    )
+    loads = {
+        key: pltpu.make_async_copy(src, dst, n.s_load.at[at])
+        for at, (key, (src, dst)) in enumerate(loads.items())
+    }
+    for copy in loads.values():
+        copy.start()
 
     def arrived(buf, count, sem):
         part = buf.at[pl.ds(0, count)]
@@ -178,14 +222,14 @@
         part = buf.at[pl.ds(0, count)]
         rcopy(part, part, sem, sem, sib).wait_send()
 
-    def arrived_heads(buf, sem):
+    def arrived_heads(buf, sem, more=0):
         @pl.when(relays)
         def _():
-            arrived(buf, 15, sem)
+            arrived(buf, 15 + more, sem)
 
         @pl.when(jnp.logical_not(relays))
         def _():
-            arrived(buf, 16, sem)
+            arrived(buf, 16 + more, sem)
 
     barrier = pltpu.get_barrier_semaphore()
     loop(
@@ -210,6 +254,16 @@
         device_id_type=MESH,
     )
 
+    loop(
+        16,
+        lambda k: pl.semaphore_signal(
+            barrier,
+            inc=1,
+            device_id={"group": g_other, "tensor": 2 * k + y},
+            device_id_type=MESH,
+        ),
+    )
+
     def f_greet(j):
         pl.semaphore_signal(
             barrier, inc=1, device_id={"group": j, "tensor": f_from}, device_id_type=MESH
@@ -221,36 +275,13 @@
     def _():
         f_greet(g)
 
-    def half(size, which):
-        return pl.ds(pl.multiple_of(size * which, size), size)
-
-    loads = dict(
-        down=(down, n.v_down),
-        x=(x, n.v_x),
-        wq=(wq, n.v_wq),
-        wk=(wk, n.v_wkv.at[pl.ds(0, 32)]),
-        wv=(wv, n.v_wkv.at[pl.ds(32, 32)]),
-        up=(up, n.v_up),
-        cot=(cot, n.v_cot),
-        hid=(hid.at[:, half(4096, c)], n.hid2.at[0]),
-        k=(kc.at[:, :, half(512, c)], n.kbuf.at[0]),
-        v=(vc.at[:, :, half(512, c)], n.vbuf.at[0]),
-        wo=(wo, n.v_wo),
-    )
-    loads = {
-        key: pltpu.make_async_copy(src, dst, n.s_load.at[at])
-        for at, (key, (src, dst)) in enumerate(loads.items())
-    }
-    for copy in loads.values():
-        copy.start()
-
     loads["down"].wait()
     n.down_own[...] = n.v_down[...].astype(BF16)
 
-    pl.semaphore_wait(barrier, 47 - f_self.astype(jnp.int32))
+    pl.semaphore_wait(barrier, 63 - f_self.astype(jnp.int32))
 
     def dn_z(k):
-        to = y * 16 + lax.rem(z + near(k), 8) * 2 + y
+        to = y * 16 + far_z(k) * 2 + y
         return rcopy(
             n.down_own, n.down_half.at[t16], n.s_dn_sz.at[0], n.s_dn_r.at[t16], tdev(to)
         )
@@ -267,7 +298,7 @@
     def dn_pass(z_of, core):
         dn_y(z_of * 2 + core, g + core * (g_other - g)).start()
 
-    loop(8, lambda k: dn_z(k).start(), 1)
+    loop(7, lambda k: dn_z(k).start())
 
     @pl.when(relays)
     def _():
@@ -276,7 +307,7 @@
 
     @pl.when(jnp.logical_not(relays))
     def _():
-        dn_z(0).start()
+        dn_z(7).start()
 
     pairs = [
         rcopy(src, dst, n.s_sib_s.at[at], n.s_sib_r.at[at], sib)
@@ -289,8 +320,7 @@
             )
         )
     ]
-    for copy in pairs:
-        copy.start()
+    pairs[0].start()
 
     loads["x"].wait()
     for s in range(4):
@@ -298,7 +328,8 @@
     xb = n.x_rows[...].astype(BF16)
     row = sublanes((16, HD))
     lane = lanes((16, HD))
-    position = (by_rollout(row & 3, start) + (row >> 2)).astype(F32)
+    loads["start"].wait()
+    position = (by_rollout(row & 3, n.start) + (row >> 2)).astype(F32)
     freq = jnp.exp((lane & 63).astype(F32) * (-math.log(rope_theta) * 2.0 / HD))
     angle = position * freq
     cosine = jnp.cos(angle)
@@ -316,38 +347,31 @@
             n.q_rows[r * 8 + h * 4 : r * 8 + h * 4 + 4, :] = rows[pl.ds(r, 4, stride=4), :]
     n.q_send[...] = n.q_rows[...].astype(BF16)
 
-    def q_copy(k):
-        i = lax.rem(i0 + k, 16)
-        return rcopy(n.q_send, n.q_buf.at[t16], n.s_q.at[0], n.s_q.at[1], tdev(2 * i + y))
-
-    @pl.when(jnp.logical_not(relays))
-    def _():
-        q_copy(0).start()
-
-    loop(16, lambda k: q_copy(k).start(), 1)
-
-    @pl.when(relays)
-    def _():
-        n.q_buf[t16] = n.q_send[...]
-
     send2 = (n.d_send2, n.u_send2)
     recv2 = (n.d_recv2, n.u_recv2)
 
     def g2(u, k):
-        j = lax.rem(g + k, 8)
+        to = far_x(k)
         return rcopy(
-            send2[u].at[j], recv2[u].at[g], n.s_g2.at[u, 0], n.s_g2.at[u, 1], gdev(j)
-        )
-
-    def g3(u, k):
-        i = lax.rem(t16 + k, 16)
+            send2[u].at[pl.ds(2 * to, 2)],
+            recv2[u].at[gx],
+            n.s_g2.at[u, 0],
+            n.s_g2.at[u, 1],
+            gdev(2 * to + gy),
+        )
+
+    def g3(u, half, k):
+        i = far_core(k)
         return rcopy(
-            n.g_send3.at[u, i], n.g_recv3.at[u, i0], n.s_g3.at[u, 0], n.s_g3.at[u, 1],
-            tdev(16 * c + i),
+            n.g_send3.at[u, half * 16 + i],
+            n.g_recv3.at[u, gy * 16 + i0],
+            n.s_g3.at[u, 0],
+            n.s_g3.at[u, 1],
+            {"group": 2 * gx + half, "tensor": 16 * c + i},
         )
 
     def g4(u, k):
-        j = lax.rem(g + k, 8)
+        j = far_group(k)
         return rcopy(
             n.g_send4.at[u], n.g_recv4.at[u, g], n.s_g4.at[u, 0], n.s_g4.at[u, 1], gdev(j)
         )
@@ -357,58 +381,65 @@
         return jnp.concatenate([first[rows], second[rows]], axis=0).astype(BF16)
 
     def stage3_out(u):
-        arrived(recv2[u], 7, n.s_g2.at[u, 1])
-        recv2[u][g] = send2[u][g]
-
-        def total(row):
+        arrived(recv2[u], 3, n.s_g2.at[u, 1])
+
+        def total(half, row):
             rows = pl.ds(pl.multiple_of(row, 16), 16)
-            sums = recv2[u][0, rows, :].astype(F32)
-            for j in range(1, 8):
-                sums = sums + recv2[u][j, rows, :].astype(F32)
+            sums = send2[u][2 * gx + half, rows, :].astype(F32)
+            for dx in range(1, 4):
+                sums = sums + recv2[u][lax.rem(gx + dx, 4), half, rows, :].astype(F32)
             return sums
 
         def send(i, low, high):
             n.g_send3[u, i] = jnp.concatenate([low, high], axis=0).astype(BF16)
 
         def down_sum(pair):
-            sums = total(pair * 16)
-            for e in range(2):
-                piece = sums[e * 8 : e * 8 + 8]
-                send(pair * 2 + e, piece[:, :128], piece[:, 128:])
+            for half in range(2):
+                sums = total(half, pair * 16)
+                for e in range(2):
+                    piece = sums[e * 8 : e * 8 + 8]
+                    send(half * 16 + pair * 2 + e, piece[:, :128], piece[:, 128:])
 
         def up_sum(part):
-            rest = total(128 + part * 16)
-            for pair in range(4):
-                sums = total(part * 64 + pair * 16)
-                high = pltpu.roll(rest, 128 - 32 * pair, 1) if pair else rest
-                for e in range(2):
-                    rows = slice(e * 8, e * 8 + 8)
-                    send(part * 8 + pair * 2 + e, sums[rows], high[rows])
+            for half in range(2):
+                rest = total(half, 128 + part * 16)
+                for pair in range(4):
+                    sums = total(half, part * 64 + pair * 16)
+                    high = pltpu.roll(rest, 128 - 32 * pair, 1) if pair else rest
+                    for e in range(2):
+                        rows = slice(e * 8, e * 8 + 8)
+                        send(half * 16 + part * 8 + pair * 2 + e, sums[rows], high[rows])
 
         if u == 0:
             loop(8, down_sum)
         else:
             loop(2, up_sum)
 
+        def both(k):
+            g3(u, 1 - gy, k).start()
+            g3(u, gy, k).start()
+
+        loop(15, both)
+        g3(u, 1 - gy, 15).start()
+
         @pl.when(jnp.logical_not(relays))
         def _():
-            g3(u, 0).start()
-
-        loop(16, lambda k: g3(u, k).start(), 1)
+            g3(u, gy, 15).start()
 
     def stage4_out(u):
-        arrived_heads(n.g_recv3.at[u], n.s_g3.at[u, 1])
+        arrived_heads(n.g_recv3.at[u], n.s_g3.at[u, 1], 16)
 
         @pl.when(relays)
         def _():
-            n.g_recv3[u, i0] = n.g_send3[u, t16]
-
-        total = n.g_recv3[u, 0].astype(F32)
-        for i in range(1, 16):
-            total = total + n.g_recv3[u, i].astype(F32)
+            n.g_recv3[u, gy * 16 + i0] = n.g_send3[u, gy * 16 + t16]
+
+        sums = [n.g_recv3[u, i].astype(F32) for i in range(4)]
+        for i in range(4, 32):
+            sums[i % 4] = sums[i % 4] + n.g_recv3[u, i].astype(F32)
+        total = (sums[0] + sums[1]) + (sums[2] + sums[3])
         n.g_send4[u] = total
         n.g_recv4[u, g] = total
-        loop(8, lambda k: g4(u, k).start(), 1)
+        loop(7, lambda k: g4(u, k).start())
         return total
 
     def summed(u):
@@ -454,7 +485,25 @@
             n.d_send2[j, rows, :] = stack8(*blocks, j)
 
     loop(8, down_pair)
-    loop(8, lambda k: g2(0, k).start(), 1)
+
+    def q_copy(k):
+        to = 2 * far_chip(k) + y
+        return rcopy(n.q_send, n.q_buf.at[t16], n.s_q.at[0], n.s_q.at[1], tdev(to))
+
+    @pl.when(jnp.logical_not(relays))
+    def _():
+        q_copy(15).start()
+
+    loop(15, lambda k: q_copy(k).start())
+
+    @pl.when(relays)
+    def _():
+        n.q_buf[t16] = n.q_send[...]
+
+    for copy in pairs[1:]:
+        copy.start()
+
+    loop(3, lambda k: g2(0, k).start())
 
     def dn_recv(slot):
         dn_y(slot, g).wait_recv()
@@ -465,14 +514,33 @@
         dn_pass(z, 1 - c)
 
         def pass_on(k):
-            from_z = lax.rem(z + near(k), 8)
+            from_z = far_z(k)
             for core in range(2):
                 dn_recv(from_z * 2 + core)
                 dn_pass(from_z, core)
 
-        loop(8, pass_on, 1)
+        loop(7, pass_on)
+
+    def reduce_part(part, total):
+        for e in range(4):
+            at = part * 4 + e
+            cols = pl.ds(pl.multiple_of(at * 256, 256), 256)
+            both = jnp.concatenate([n.hid2[0, :, cols], n.hid2[1, :, cols]], axis=0)
+            total = total + dot(n.down_half[at], both, NT)
+        return total
+
+    pt = rcopy(n.part_send, n.part_recv, n.s_pt.at[0], n.s_pt.at[1], sib)
+
+    def reduce():
+        n.part_send[...] = lax.fori_loop(0, 4, reduce_part, jnp.zeros((64, 256), F32))
+        pt.start()
+
+    @pl.when(relays)
+    def _():
+        reduce()
 
     arrived_heads(n.q_buf, n.s_q.at[1])
+    loads["fill"].wait()
     loads["k"].wait()
     loads["v"].wait()
     pairs[1].wait_recv()
@@ -482,7 +550,22 @@
     spot = jnp.where(spot < 128, t * 128 + spot, (t + 1 - 2 * c) * 128 + spot - 128)
     tile_lane = lanes((8, 128))
 
-    def attend(kk):
+    def send_part(i):
+        to = tdev(16 * c + i)
+        stays = relays & (i == t16)
+
+        @pl.when(jnp.logical_not(stays))
+        def _():
+            rcopy(n.a_send.at[i], n.a_recv.at[i0], n.s_a.at[0], n.s_a.at[1], to).start()
+            rcopy(n.l_send.at[i], n.l_recv.at[i0], n.s_l.at[0], n.s_l.at[1], to).start()
+
+        @pl.when(stays)
+        def _():
+            n.a_recv[i0] = n.a_send[i]
+            n.l_recv[i0] = n.l_send[i]
+
+    def attend(step):
+        kk = lax.rem(step + 2 + lax.div(z, 2), 4)
         cols = pl.ds(pl.multiple_of(kk * HD, HD), HD)
         qs = [n.q_buf[kk * 4 + j].astype(F32) for j in range(4)]
         outs, tops, sums = [], [], []
@@ -490,7 +573,7 @@
             qr = jnp.concatenate([a[r * 8 : r * 8 + 8] for a in qs], axis=0).astype(BF16)
             keys = jnp.concatenate([n.kbuf[0, r, :, cols], n.kbuf[1, r, :, cols]], axis=0)
             values = jnp.concatenate([n.vbuf[0, r, :, cols], n.vbuf[1, r, :, cols]], axis=0)
-            valid = spot < fill[r]
+            valid = spot < n.fill[r]
             scores = jnp.where(valid, dot(qr, keys, NT) * INV_ROOT, masked_score)
             top = jnp.max(scores, axis=1, keepdims=True)
             weights = jnp.where(valid, jnp.exp(scores - top), 0.0)
@@ -505,50 +588,18 @@
                 tile = jnp.where(tile_lane == r, tops[r][rows], tile)
                 tile = jnp.where(tile_lane == 64 + r, sums[r][rows], tile)
             n.l_send[kk * 4 + j] = tile
-
-    loop(2, attend)
+        for j in range(4):
+            send_part(kk * 4 + j)
+
+    loop(1, attend)
+
+    stage3_out(0)
+    loop(2, attend, 1)
 
     @pl.when(jnp.logical_not(relays))
     def _():
         loop(16, dn_recv)
-
-    def reduce_part(part, total):
-        for e in range(4):
-            at = part * 4 + e
-            cols = pl.ds(pl.multiple_of(at * 256, 256), 256)
-            both = jnp.concatenate([n.hid2[0, :, cols], n.hid2[1, :, cols]], axis=0)
-            total = total + dot(n.down_half[at], both, NT)
-        return total
-
-    n.part_send[...] = lax.fori_loop(0, 4, reduce_part, jnp.zeros((64, 256), F32))
-    pt = rcopy(n.part_send, n.part_recv, n.s_pt.at[0], n.s_pt.at[1], sib)
-    pt.start()
-
-    stage3_out(0)
-    loop(4, attend, 2)
-
-    def a_copy(k):
-        i = lax.rem(t16 + k, 16)
-        to = tdev(16 * c + i)
-        return (
-            rcopy(n.a_send.at[i], n.a_recv.at[i0], n.s_a.at[0], n.s_a.at[1], to),
-            rcopy(n.l_send.at[i], n.l_recv.at[i0], n.s_l.at[0], n.s_l.at[1], to),
-        )
-
-    def a_start(k):
-        for copy in a_copy(k):
-            copy.start()
-
-    @pl.when(jnp.logical_not(relays))
-    def _():
-        a_start(0)
-
-    loop(16, a_start, 1)
-
-    @pl.when(relays)
-    def _():
-        n.a_recv[i0] = n.a_send[t16]
-        n.l_recv[i0] = n.l_send[t16]
+        reduce()
 
     pt.wait_recv()
     pairs[3].wait_recv()
@@ -589,7 +640,9 @@
             n.u_send2[j, rows, :] = stack8(*rest, j)
 
     loop(2, up_part)
-    loop(8, lambda k: g2(1, k).start(), 1)
+    loop(3, lambda k: g2(1, k).start())
+
+    loop(4, attend, 2)
 
     arrived(n.n_buf, 3, n.s_n.at[1])
     fresh = [n.n_buf[j].astype(F32) for j in range(4)]
@@ -617,12 +670,12 @@
         new_total = jnp.where(tile_lane == r, new_sum[rows], new_total)
 
     stage4_out(0)
+    stage3_out(1)
+
     arrived_heads(n.a_recv, n.s_a.at[1])
     arrived_heads(n.l_recv, n.s_l.at[1])
 
-    stage3_out(1)
-
-    peak = lax.fori_loop(0, 16, lambda i, m: jnp.maximum(m, n.l_recv[i]), new_tile)
+    peak = lax.fori_loop(0, 16, lambda i, m: jnp.maximum(m, n.l_recv[i]), new_tile, unroll=True)
     scale = jnp.exp(new_tile - peak)
 
     def join(i, state):
@@ -643,6 +696,7 @@
             scale * new_total,
             [new_out[r * 8 : r * 8 + 8] * scale[:, r : r + 1] for r in range(4)],
         ),
+        unroll=4,
     )
     for r in range(4):
         n.q_rows[r * 8 : r * 8 + 8, :] = parts[r] / total[:, r : r + 1]
@@ -696,12 +750,12 @@
     loop(16, out_sum)
 
     def o2(k):
-        i = lax.rem(i0 + k, 16)
+        i = far_chip(k)
         return rcopy(
             n.o_send2.at[i], n.o_recv2.at[i0], n.s_o2.at[0], n.s_o2.at[1], tdev(2 * i + c)
         )
 
-    loop(16, lambda k: o2(k).start(), 1)
+    loop(15, lambda k: o2(k).start())
 
     up_total = stage4_out(1)
     up_total = jnp.concatenate([up_total[:8], up_total[8:]], axis=1)
@@ -724,14 +778,14 @@
     def _():
         n.f_recv[g] = n.f_send[f_own]
 
-    def left_heads(buf, sem):
+    def left_heads(buf, sem, more=0):
         @pl.when(relays)
         def _():
-            left(buf, 15, sem)
+            left(buf, 15 + more, sem)
 
         @pl.when(jnp.logical_not(relays))
         def _():
-            left(buf, 16, sem)
+            left(buf, 16 + more, sem)
 
     @pl.when(relays)
     def _():
@@ -750,9 +804,9 @@
     pt.wait_send()
     left_heads(n.a_send, n.s_a.at[0])
     left_heads(n.l_send, n.s_l.at[0])
-    left(n.d_send2, 7, n.s_g2.at[0, 0])
-    left(n.u_send2, 7, n.s_g2.at[1, 0])
-    left_heads(n.g_send3.at[0], n.s_g3.at[0, 0])
+    left(n.d_recv2, 3, n.s_g2.at[0, 0])
+    left(n.u_recv2, 3, n.s_g2.at[1, 0])
+    left_heads(n.g_send3.at[0], n.s_g3.at[0, 0], 16)
     left(n.g_recv4.at[0], 7, n.s_g4.at[0, 0])
 
     first_col = 160 * t
@@ -770,8 +824,9 @@
     )
     low = jnp.where(lane < 64, 0.0, total[:, 128:]).astype(BF16)
     decoded = total + adapter_scale * dot(low, n.fu_pad[...])
+    loads["live"].wait()
     wide_row = sublanes((16, 256))
-    alive = (wide_row >> 2) < by_rollout(wide_row & 3, live)
+    alive = (wide_row >> 2) < by_rollout(wide_row & 3, n.live)
     n.d_rows[...] = jnp.where(alive, decoded, 0.0)
     for s in range(4):
         n.w_dec[s] = n.d_rows[s * 4 : s * 4 + 4, 0:160].astype(BF16)
@@ -794,7 +849,7 @@
     n.w_fu[...] = jnp.concatenate([piece, piece], axis=0).T[0:20, 0:64]
     results[2].start()
 
-    left_heads(n.g_send3.at[1], n.s_g3.at[1, 0])
+    left_heads(n.g_send3.at[1], n.s_g3.at[1, 0], 16)
     left(n.g_recv4.at[1], 7, n.s_g4.at[1, 0])
     o1.wait_send()
     left(n.o_send2, 15, n.s_o2.at[0])
@@ -819,7 +874,6 @@
 
 def body(hid, cot, down, up, wo, wq, wk, wv, x, kc, vc, fill, start, live):
     hbm = pl.BlockSpec(memory_space=pl.ANY)
-    smem = pl.BlockSpec(memory_space=pltpu.SMEM)
     vmem = pl.BlockSpec(memory_space=pltpu.VMEM)
     shapes = (
         jax.ShapeDtypeStruct((4, 4, 160), BF16),
@@ -829,9 +883,10 @@
     results = pl.pallas_call(
         kernel,
         out_shape=shapes,
-        in_specs=[hbm] * 11 + [smem] * 3,
+        in_specs=[hbm] * 14,
         out_specs=(hbm,) * 3,
         scratch_shapes=[pltpu.VMEM(shape, kind) for shape, kind in SCRATCH.values()]
+        + [pltpu.SMEM((4,), jnp.int32)] * 3
         + [pltpu.SemaphoreType.DMA(shape) for shape in SEMS.values()],
         compiler_params=pltpu.CompilerParams(
             collective_id=0, has_side_effects=True, vmem_limit_bytes=56 * 2**20

time: 55.8 us -> 51.5 us (0.923)
  Pallas kernels: 55.1 us -> 50.7 us
    pallas_call x1, Pallas kernels: 53.6 us -> 49.2 us  [body(): pl.pallas_call(kernel, out_shape=shapes, in_specs=[hbm] * 14, out_specs=(...]
where the time goes in v3:
time: 51.5 us; the launch traced here: 51.4 us
  Pallas kernels  50.7 us (98%)
  between operations  0.64 us (1%)
    pallas_call x1, Pallas kernels, body(): pl.pallas_call(kernel, out_shape=shapes, in_specs=[hbm] * 14, out_specs=(...  49.2 us
    pallas_call x1, Pallas kernels, body(): pl.pallas_call(hand_out, out_shape=shapes, in_specs=[vmem] * 3, out_specs...  1.48 us

profile of v3, /device:TPU:3, one launch (start us, length us, event | category | flops | bytes accessed | tf_op | source)
XLA Modules:
  0.0 51.4 jit_solution(3363313858298816845)
XLA Ops:
  0.6 49.2 %update_and_decode.1 = (bf16[4,4,160]{2,1,0:T(4,128)(2,1)}, f32[64,256]{1,0:T(8,128)}, f32[20,64]{1,0:T(8,128)}) custom-call(bf16[128,8192]{1,0:T(8,128)(2,1)} %hid.1, bf16[128,5120]{1,0:T(8,128)(2,1)} %cot.1, f32[64,256]{1,0:T(8,128)} %bitcast.7, f32[64,5120]{1,0:T(8,128)} %up.1, bf16[256,5120]{1,0:T(8,128)(2,1)} %wo.1, bf16[5120,256]{1,0:T(8,128)(2,1)} %wq.1, ...), custom_call_target="tpu_custom_call" | custom-call | tf_op jit(solution)/shard_map/update_and_decode/pallas_call | solution.py:883
  49.9 1.5 %hand_out.1 = (bf16[4,4,160]{2,1,0:T(4,128)(2,1)}, f32[64,256]{1,0:T(8,128)}, f32[20,64]{1,0:T(8,128)}) custom-call(bf16[4,4,160]{2,1,0:T(4,128)(2,1)} %get-tuple-element.9.dec, f32[64,256]{1,0:T(8,128)} %get-tuple-element.10.fd, f32[20,64]{1,0:T(8,128)} %get-tuple-element.11.fu), custom_call_target="tpu_custom_call" | custom-call | tf_op jit(solution)/shard_map/hand_out/pallas_call | solution.py:896

commit v4 on v3

--- a/solution.py
+++ b/solution.py
@@ -41,6 +41,11 @@
         return carry
 
     lax.fori_loop(start, n, step, 0)
+
+
+def each(n, fn, start=0):
+    for k in range(start, n):
+        fn(k)
 
 
 SCRATCH = dict(
@@ -53,7 +58,10 @@
     v_cot=((128, 5120), BF16),
     cot2=((128, 2560), BF16),
     hid2=((2, 128, 4096), BF16),
-    v_wo=((256, 5120), BF16),
+    wo2=((2, 256, 2560), BF16),
+    att2=((2, 16, 256), BF16),
+    t_send=((16, 128), F32),
+    t_recv=((16, 128), F32),
     kbuf=((2, 4, 128, 512), BF16),
     vbuf=((2, 4, 128, 512), BF16),
     down_own=((64, 256), BF16),
@@ -81,12 +89,10 @@
     g_send4=((2, 16, 128), F32),
     g_recv4=((2, 8, 16, 128), F32),
     u_tmp=((64, 1280), F32),
-    p_rows=((16, 5120), F32),
+    p_rows=((16, 2560), F32),
     fd_pad=((128, 256), BF16),
     fu_pad=((128, 256), BF16),
-    o_send1=((16, 16, 256), BF16),
     o_keep=((16, 16, 256), F32),
-    o_recv1=((16, 16, 256), BF16),
     o_send2=((16, 16, 256), BF16),
     o_recv2=((16, 16, 256), BF16),
     d_rows=((16, 256), F32),
@@ -101,8 +107,8 @@
     dn_sz=(1,),
     dn_sy=(1,),
     dn_r=(16,),
-    sib_s=(4,),
-    sib_r=(4,),
+    sib_s=(5,),
+    sib_r=(5,),
     bk=(2,),
     pt=(2,),
     q=(2,),
@@ -112,7 +118,8 @@
     g2=(2, 2),
     g3=(2, 2),
     g4=(2, 2),
-    o1=(2,),
+    at=(2,),
+    tt=(2,),
     o2=(2,),
     f=(2,),
     out=(3,),
@@ -163,24 +170,20 @@
     def gdev(index):
         return {"group": index}
 
-    def near(k):
-        return lax.rem(lax.div(k + 1, 2) * (7 - 6 * lax.rem(k, 2)), 8)
-
     def far_z(k):
-        return lax.rem(z + near(7 - k), 8)
+        return lax.rem(z + (4, 5, 3, 6, 2, 7, 1, 0)[k], 8)
 
     def far_core(k):
-        return far_z(lax.div(k, 2)) * 2 + lax.rem(c + 1 + k, 2)
+        return far_z(k // 2) * 2 + (c if k % 2 else 1 - c)
 
     def far_chip(k):
-        return lax.rem(y + 1 + k, 2) * 8 + far_z(lax.div(k, 2))
+        return (y if k % 2 else 1 - y) * 8 + far_z(k // 2)
 
     def far_x(k):
-        at = 3 - k
-        return lax.rem(gx + lax.div(at + 1, 2) * (3 - 2 * lax.rem(at, 2)), 4)
+        return lax.rem(gx + (2, 3, 1, 0)[k], 4)
 
     def far_group(k):
-        return far_x(lax.rem(k, 4)) * 2 + lax.rem(g + 1 - lax.div(k, 4), 2)
+        return far_x(k % 4) * 2 + (1 - gy if k < 4 else gy)
 
     f_from = 4 * g + lax.div(t, 8)
     f_self = f_from == t
@@ -202,7 +205,7 @@
         hid=(hid.at[:, half(4096, c)], n.hid2.at[0]),
         k=(kc.at[:, :, half(512, c)], n.kbuf.at[0]),
         v=(vc.at[:, :, half(512, c)], n.vbuf.at[0]),
-        wo=(wo, n.v_wo),
+        wo=(wo.at[:, half(2560, c)], n.wo2.at[0]),
         start=(start_in, n.start),
         fill=(fill_in, n.fill),
         live=(live_in, n.live),
@@ -232,14 +235,14 @@
             arrived(buf, 16 + more, sem)
 
     barrier = pltpu.get_barrier_semaphore()
-    loop(
+    each(
         32,
         lambda k: pl.semaphore_signal(
             barrier, inc=1, device_id=tdev(lax.rem(t + k, 32)), device_id_type=MESH
         ),
         1,
     )
-    loop(
+    each(
         8,
         lambda k: pl.semaphore_signal(
             barrier, inc=1, device_id=gdev(lax.rem(g + k, 8)), device_id_type=MESH
@@ -254,7 +257,7 @@
         device_id_type=MESH,
     )
 
-    loop(
+    each(
         16,
         lambda k: pl.semaphore_signal(
             barrier,
@@ -269,7 +272,7 @@
             barrier, inc=1, device_id={"group": j, "tensor": f_from}, device_id_type=MESH
         )
 
-    loop(8, lambda k: f_greet(lax.rem(g + k, 8)), 1)
+    each(8, lambda k: f_greet(lax.rem(g + k, 8)), 1)
 
     @pl.when(jnp.logical_not(f_self))
     def _():
@@ -298,7 +301,7 @@
     def dn_pass(z_of, core):
         dn_y(z_of * 2 + core, g + core * (g_other - g)).start()
 
-    loop(7, lambda k: dn_z(k).start())
+    each(7, lambda k: dn_z(k).start())
 
     @pl.when(relays)
     def _():
@@ -317,6 +320,7 @@
                 (kc.at[:, :, half(512, 1 - c)], n.kbuf.at[1]),
                 (vc.at[:, :, half(512, 1 - c)], n.vbuf.at[1]),
                 (cot.at[:, half(2560, 1 - c)], n.cot2),
+                (wo.at[:, half(2560, 1 - c)], n.wo2.at[1]),
             )
         )
     ]
@@ -350,11 +354,13 @@
     send2 = (n.d_send2, n.u_send2)
     recv2 = (n.d_recv2, n.u_recv2)
 
-    def g2(u, k):
+    def g2(u, part, k):
         to = far_x(k)
+        size = (64, 80)[u]
+        rows = pl.ds(part * size, size)
         return rcopy(
-            send2[u].at[pl.ds(2 * to, 2)],
-            recv2[u].at[gx],
+            send2[u].at[pl.ds(2 * to, 2), rows],
+            recv2[u].at[gx, :, rows],
             n.s_g2.at[u, 0],
             n.s_g2.at[u, 1],
             gdev(2 * to + gy),
@@ -402,9 +408,9 @@
 
         def up_sum(part):
             for half in range(2):
-                rest = total(half, 128 + part * 16)
+                rest = total(half, part * 80 + 64)
                 for pair in range(4):
-                    sums = total(half, part * 64 + pair * 16)
+                    sums = total(half, part * 80 + pair * 16)
                     high = pltpu.roll(rest, 128 - 32 * pair, 1) if pair else rest
                     for e in range(2):
                         rows = slice(e * 8, e * 8 + 8)
@@ -419,7 +425,7 @@
             g3(u, 1 - gy, k).start()
             g3(u, gy, k).start()
 
-        loop(15, both)
+        each(15, both)
         g3(u, 1 - gy, 15).start()
 
         @pl.when(jnp.logical_not(relays))
@@ -439,8 +445,10 @@
         total = (sums[0] + sums[1]) + (sums[2] + sums[3])
         n.g_send4[u] = total
         n.g_recv4[u, g] = total
-        loop(7, lambda k: g4(u, k).start())
         return total
+
+    def stage4_send(u):
+        each(7, lambda k: g4(u, k).start())
 
     def summed(u):
         arrived(n.g_recv4.at[u], 7, n.s_g4.at[u, 1])
@@ -465,7 +473,7 @@
         to = t - b4 + lax.rem(b4 + k, 4)
         return rcopy(n.n_send, n.n_buf.at[b4], n.s_n.at[0], n.s_n.at[1], tdev(to))
 
-    loop(4, lambda k: n_copy(k).start(), 1)
+    each(4, lambda k: n_copy(k).start(), 1)
     n.n_buf[b4] = n.n_send[...]
 
     loads["hid"].wait()
@@ -484,7 +492,9 @@
         for j in range(8):
             n.d_send2[j, rows, :] = stack8(*blocks, j)
 
-    loop(8, down_pair)
+    for part in range(2):
+        loop(part * 4 + 4, down_pair, part * 4)
+        each(3, lambda k: g2(0, part, k).start())
 
     def q_copy(k):
         to = 2 * far_chip(k) + y
@@ -494,7 +504,7 @@
     def _():
         q_copy(15).start()
 
-    loop(15, lambda k: q_copy(k).start())
+    each(15, lambda k: q_copy(k).start())
 
     @pl.when(relays)
     def _():
@@ -502,8 +512,6 @@
 
     for copy in pairs[1:]:
         copy.start()
-
-    loop(3, lambda k: g2(0, k).start())
 
     def dn_recv(slot):
         dn_y(slot, g).wait_recv()
@@ -519,25 +527,34 @@
                 dn_recv(from_z * 2 + core)
                 dn_pass(from_z, core)
 
-        loop(7, pass_on)
-
-    def reduce_part(part, total):
-        for e in range(4):
-            at = part * 4 + e
-            cols = pl.ds(pl.multiple_of(at * 256, 256), 256)
-            both = jnp.concatenate([n.hid2[0, :, cols], n.hid2[1, :, cols]], axis=0)
-            total = total + dot(n.down_half[at], both, NT)
-        return total
+        each(7, pass_on)
+
+    def reduce_slice(at, total):
+        cols = pl.ds(pl.multiple_of(at * 256, 256), 256)
+        both = jnp.concatenate([n.hid2[0, :, cols], n.hid2[1, :, cols]], axis=0)
+        return total + dot(n.down_half[at], both, NT)
 
     pt = rcopy(n.part_send, n.part_recv, n.s_pt.at[0], n.s_pt.at[1], sib)
 
-    def reduce():
-        n.part_send[...] = lax.fori_loop(0, 4, reduce_part, jnp.zeros((64, 256), F32))
+    @pl.when(relays)
+    def _():
+        total = jnp.zeros((64, 256), F32)
+        for at in range(16):
+            total = reduce_slice(at, total)
+        n.part_send[...] = total
         pt.start()
 
-    @pl.when(relays)
-    def _():
-        reduce()
+    @pl.when(jnp.logical_not(relays))
+    def _():
+        total = jnp.zeros((64, 256), F32)
+        for k in (7, 0, 1, 2, 3, 4, 5, 6):
+            slices = [far_z(k) * 2 + core for core in range(2)]
+            for at in slices:
+                dn_recv(at)
+            for at in slices:
+                total = reduce_slice(at, total)
+        n.part_send[...] = total
+        pt.start()
 
     arrived_heads(n.q_buf, n.s_q.at[1])
     loads["fill"].wait()
@@ -546,7 +563,7 @@
     pairs[1].wait_recv()
     pairs[2].wait_recv()
 
-    spot = lanes((32, 256))
+    spot = lanes((64, 256))
     spot = jnp.where(spot < 128, t * 128 + spot, (t + 1 - 2 * c) * 128 + spot - 128)
     tile_lane = lanes((8, 128))
 
@@ -564,13 +581,30 @@
             n.a_recv[i0] = n.a_send[i]
             n.l_recv[i0] = n.l_send[i]
 
+    def pair_at(step):
+        return lax.rem(step + 1 + lax.div(z, 4), 2)
+
+    def send_parts(step):
+        each(8, lambda j: send_part(pair_at(step) * 8 + j))
+
     def attend(step):
-        kk = lax.rem(step + 2 + lax.div(z, 2), 4)
-        cols = pl.ds(pl.multiple_of(kk * HD, HD), HD)
-        qs = [n.q_buf[kk * 4 + j].astype(F32) for j in range(4)]
+        pair = pair_at(step)
+        cols = pl.ds(pl.multiple_of(pair * 256, 256), 256)
+        qs = [n.q_buf[pair * 8 + j].astype(F32) for j in range(8)]
+        none = jnp.zeros((32, 128), F32)
         outs, tops, sums = [], [], []
         for r in range(4):
-            qr = jnp.concatenate([a[r * 8 : r * 8 + 8] for a in qs], axis=0).astype(BF16)
+            first, second = (
+                jnp.concatenate([a[r * 8 : r * 8 + 8] for a in qs[h * 4 : h * 4 + 4]], axis=0)
+                for h in range(2)
+            )
+            qr = jnp.concatenate(
+                [
+                    jnp.concatenate([first, none], axis=1),
+                    jnp.concatenate([none, second], axis=1),
+                ],
+                axis=0,
+            ).astype(BF16)
             keys = jnp.concatenate([n.kbuf[0, r, :, cols], n.kbuf[1, r, :, cols]], axis=0)
             values = jnp.concatenate([n.vbuf[0, r, :, cols], n.vbuf[1, r, :, cols]], axis=0)
             valid = spot < n.fill[r]
@@ -580,26 +614,29 @@
             tops.append(top)
             sums.append(jnp.sum(weights, axis=1, keepdims=True))
             outs.append(dot(weights.astype(BF16), values))
-        for j in range(4):
+        for j in range(8):
             rows = slice(j * 8, j * 8 + 8)
-            n.a_send[kk * 4 + j] = jnp.concatenate([o[rows] for o in outs], axis=0).astype(BF16)
+            half = slice(j // 4 * 128, j // 4 * 128 + 128)
+            n.a_send[pair * 8 + j] = jnp.concatenate(
+                [o[rows, half] for o in outs], axis=0
+            ).astype(BF16)
             tile = jnp.zeros((8, 128), F32)
             for r in range(4):
                 tile = jnp.where(tile_lane == r, tops[r][rows], tile)
                 tile = jnp.where(tile_lane == 64 + r, sums[r][rows], tile)
-            n.l_send[kk * 4 + j] = tile
-        for j in range(4):
-            send_part(kk * 4 + j)
+            n.l_send[pair * 8 + j] = tile
 
     loop(1, attend)
 
     stage3_out(0)
-    loop(2, attend, 1)
-
-    @pl.when(jnp.logical_not(relays))
-    def _():
-        loop(16, dn_recv)
-        reduce()
+    send_parts(0)
+
+    until = jnp.where(relays, 2, 1)
+    def attend_and_send(step):
+        attend(step)
+        send_parts(step)
+
+    loop(until, attend_and_send, 1)
 
     pt.wait_recv()
     pairs[3].wait_recv()
@@ -615,7 +652,7 @@
         both = jnp.concatenate(
             [
                 n.v_cot[:, pl.ds(pl.multiple_of(2560 * c + 1280 * part, 1280), 1280)],
-                n.cot2[:, pl.ds(pl.multiple_of(1280 * part, 1280), 1280)],
+                n.cot2[:, pl.ds(1280 * part, 1280)],
             ],
             axis=0,
         )
@@ -632,17 +669,17 @@
                 low.append(window[:, :128])
                 high = pltpu.roll(window[:, 128:], 32 * pair, 1) if pair else window[:, 128:]
                 rest[e] = jnp.where(quarter == pair, high, rest[e])
-            rows = pl.ds(pl.multiple_of(part * 64 + pair * 16, 16), 16)
+            rows = pl.ds(part * 80 + pair * 16, 16)
             for j in range(8):
                 n.u_send2[j, rows, :] = stack8(*low, j)
-        rows = pl.ds(pl.multiple_of(128 + part * 16, 16), 16)
+        rows = pl.ds(part * 80 + 64, 16)
         for j in range(8):
             n.u_send2[j, rows, :] = stack8(*rest, j)
-
-    loop(2, up_part)
-    loop(3, lambda k: g2(1, k).start())
-
-    loop(4, attend, 2)
+        each(3, lambda k: g2(1, part, k).start())
+
+    each(2, up_part)
+
+    loop(2, attend_and_send, until)
 
     arrived(n.n_buf, 3, n.s_n.at[1])
     fresh = [n.n_buf[j].astype(F32) for j in range(4)]
@@ -670,6 +707,7 @@
         new_total = jnp.where(tile_lane == r, new_sum[rows], new_total)
 
     stage4_out(0)
+    stage4_send(0)
     stage3_out(1)
 
     arrived_heads(n.a_recv, n.s_a.at[1])
@@ -704,8 +742,23 @@
         for r in range(4):
             rows[pl.ds(r, 4, stride=4), :] = n.q_rows[r * 8 + h * 4 : r * 8 + h * 4 + 4, :]
     att = jnp.concatenate([n.q_rot0[...], n.q_rot1[...]], axis=1).astype(BF16)
+    n.att2[0] = att
+    at = rcopy(n.att2.at[0], n.att2.at[1], n.s_at.at[0], n.s_at.at[1], sib)
+    at.start()
     loads["wo"].wait()
-    n.p_rows[...] = dot(att, n.v_wo[...])
+    pairs[4].wait_recv()
+    at.wait_recv()
+    n.p_rows[...] = dot(n.att2[0], n.wo2[0]) + dot(n.att2[1], n.wo2[1])
+
+    def out_part(part):
+        for e in range(8):
+            at = 160 * e // 128 * 128
+            shift = 160 * e - at
+            base = pl.multiple_of(part * 1280 + at, 128)
+            window = n.p_rows[:, pl.ds(base, 256)]
+            n.o_keep[part * 8 + e] = pltpu.roll(window, 256 - shift, 1) if shift else window
+
+    loop(2, out_part)
 
     fd = n.v_down[...] - STEP_SCALE * summed(0)
     n.w_fd[...] = fd
@@ -718,44 +771,31 @@
     results[1].start()
     n.fd_pad[0:64, :] = jnp.zeros((64, 256), BF16)
     n.fd_pad[64:128, :] = fd.astype(BF16)
-    low = dot(att, n.fd_pad[...], NT)
-
-    o1 = rcopy(n.o_send1, n.o_recv1, n.s_o1.at[0], n.s_o1.at[1], sib)
-
-    def out_part(part):
-        for pair in range(4):
-            both = []
-            for e in (pair * 2, pair * 2 + 1):
-                at = 160 * e // 128 * 128
-                shift = 160 * e - at
-                base = pl.multiple_of(part * 1280 + at, 128)
-                window = n.p_rows[:, pl.ds(base, 256)]
-                window = pltpu.roll(window, 256 - shift, 1) if shift else window
-                both.append(
-                    jnp.concatenate(
-                        [window[:, :128], jnp.where(lane < 32, window[:, 128:], low)], axis=1
-                    )
-                )
-            n.o_send1[part * 4 + pair] = jnp.where(c == 0, both[1], both[0]).astype(BF16)
-            n.o_keep[part * 4 + pair] = jnp.where(c == 0, both[0], both[1])
-
-    loop(4, out_part)
-    o1.start()
-
-    o1.wait_recv()
+    n.t_send[...] = dot(att, n.fd_pad[...], NT)
+    tt = rcopy(n.t_send, n.t_recv, n.s_tt.at[0], n.s_tt.at[1], sib)
+    tt.start()
+
+    def o2(k):
+        i = far_core(k)
+        return rcopy(
+            n.o_send2.at[i], n.o_recv2.at[i0], n.s_o2.at[0], n.s_o2.at[1], tdev(16 * c + i)
+        )
+
+    tt.wait_recv()
+    low = n.t_send[...] + n.t_recv[...]
 
     def out_sum(i):
-        n.o_send2[i] = (n.o_keep[i] + n.o_recv1[i].astype(F32)).astype(BF16)
-
-    loop(16, out_sum)
-
-    def o2(k):
-        i = far_chip(k)
-        return rcopy(
-            n.o_send2.at[i], n.o_recv2.at[i0], n.s_o2.at[0], n.s_o2.at[1], tdev(2 * i + c)
-        )
-
-    loop(15, lambda k: o2(k).start())
+        part = n.o_keep[i]
+        n.o_send2[i] = jnp.concatenate(
+            [part[:, :128], jnp.where(lane < 32, part[:, 128:], low)], axis=1
+        ).astype(BF16)
+
+    lax.fori_loop(0, 16, lambda i, a: (out_sum(i), a)[1], 0, unroll=4)
+    each(15, lambda k: o2(k).start())
+
+    @pl.when(jnp.logical_not(relays))
+    def _():
+        o2(15).start()
 
     up_total = stage4_out(1)
     up_total = jnp.concatenate([up_total[:8], up_total[8:]], axis=1)
@@ -772,11 +812,12 @@
         def _():
             f_copy(e).start()
 
-    loop(8, f_start)
+    each(8, f_start)
 
     @pl.when(f_self)
     def _():
         n.f_recv[g] = n.f_send[f_own]
+    stage4_send(1)
 
     def left_heads(buf, sem, more=0):
         @pl.when(relays)
@@ -817,10 +858,13 @@
     n.fu_pad[0:64, :] = jnp.zeros((64, 256), BF16)
     n.fu_pad[64:128, :] = fu.astype(BF16)
 
-    arrived(n.o_recv2, 15, n.s_o2.at[1])
-    n.o_recv2[i0] = n.o_send2[i0]
+    arrived_heads(n.o_recv2, n.s_o2.at[1])
+    @pl.when(relays)
+    def _():
+        n.o_recv2[i0] = n.o_send2[t16]
+
     total = lax.fori_loop(
-        1, 16, lambda i, a: a + n.o_recv2[i].astype(F32), n.o_recv2[0].astype(F32)
+        1, 16, lambda i, a: a + n.o_recv2[i].astype(F32), n.o_recv2[0].astype(F32), unroll=5
     )
     low = jnp.where(lane < 64, 0.0, total[:, 128:]).astype(BF16)
     decoded = total + adapter_scale * dot(low, n.fu_pad[...])
@@ -851,8 +895,9 @@
 
     left_heads(n.g_send3.at[1], n.s_g3.at[1, 0], 16)
     left(n.g_recv4.at[1], 7, n.s_g4.at[1, 0])
-    o1.wait_send()
-    left(n.o_send2, 15, n.s_o2.at[0])
+    at.wait_send()
+    tt.wait_send()
+    left_heads(n.o_send2, n.s_o2.at[0])
 
     @pl.when(f_self)
     def _():

time: 51.5 us -> 49.7 us (0.965)
  Pallas kernels: 50.7 us -> 48.9 us
    pallas_call x1, Pallas kernels: 49.2 us -> 47.4 us  [body(): pl.pallas_call(kernel, out_shape=shapes, in_specs=[hbm] * 14, out_specs=(...]
where the time goes in v4:
time: 49.7 us; the launch traced here: 49.6 us
  Pallas kernels  48.9 us (98%)
  between operations  0.64 us (1%)
    pallas_call x1, Pallas kernels, body(): pl.pallas_call(kernel, out_shape=shapes, in_specs=[hbm] * 14, out_specs=(...  47.4 us
    pallas_call x1, Pallas kernels, body(): pl.pallas_call(hand_out, out_shape=shapes, in_specs=[vmem] * 3, out_specs...  1.48 us

profile of v4, /device:TPU:3, one launch (start us, length us, event | category | flops | bytes accessed | tf_op | source)
XLA Modules:
  0.0 49.6 jit_solution(761739003283322618)
XLA Ops:
  0.6 47.4 %update_and_decode.1 = (bf16[4,4,160]{2,1,0:T(4,128)(2,1)}, f32[64,256]{1,0:T(8,128)}, f32[20,64]{1,0:T(8,128)}) custom-call(bf16[128,8192]{1,0:T(8,128)(2,1)} %hid.1, bf16[128,5120]{1,0:T(8,128)(2,1)} %cot.1, f32[64,256]{1,0:T(8,128)} %bitcast.7, f32[64,5120]{1,0:T(8,128)} %up.1, bf16[256,5120]{1,0:T(8,128)(2,1)} %wo.1, bf16[5120,256]{1,0:T(8,128)(2,1)} %wq.1, ...), custom_call_target="tpu_custom_call" | custom-call | tf_op jit(solution)/shard_map/update_and_decode/pallas_call | solution.py:928
  48.1 1.5 %hand_out.1 = (bf16[4,4,160]{2,1,0:T(4,128)(2,1)}, f32[64,256]{1,0:T(8,128)}, f32[20,64]{1,0:T(8,128)}) custom-call(bf16[4,4,160]{2,1,0:T(4,128)(2,1)} %get-tuple-element.9.dec, f32[64,256]{1,0:T(8,128)} %get-tuple-element.10.fd, f32[20,64]{1,0:T(8,128)} %get-tuple-element.11.fu), custom_call_target="tpu_custom_call" | custom-call | tf_op jit(solution)/shard_map/hand_out/pallas_call | solution.py:941

commit v5 on v4

--- a/solution.py
+++ b/solution.py
@@ -235,13 +235,14 @@
             arrived(buf, 16 + more, sem)
 
     barrier = pltpu.get_barrier_semaphore()
-    each(
-        32,
-        lambda k: pl.semaphore_signal(
+    def t_greet(k):
+        pl.semaphore_signal(
             barrier, inc=1, device_id=tdev(lax.rem(t + k, 32)), device_id_type=MESH
-        ),
-        1,
-    )
+        )
+
+    near = (1, 31, 16, 15, 17)
+    for k in near:
+        t_greet(k)
     each(
         8,
         lambda k: pl.semaphore_signal(
@@ -277,6 +278,10 @@
     @pl.when(jnp.logical_not(f_self))
     def _():
         f_greet(g)
+
+    for k in range(1, 32):
+        if k not in near:
+            t_greet(k)
 
     loads["down"].wait()
     n.down_own[...] = n.v_down[...].astype(BF16)
@@ -706,10 +711,10 @@
         new_tile = jnp.where(tile_lane == r, new_top[rows], new_tile)
         new_total = jnp.where(tile_lane == r, new_sum[rows], new_total)
 
+    stage3_out(1)
+
     stage4_out(0)
     stage4_send(0)
-    stage3_out(1)
-
     arrived_heads(n.a_recv, n.s_a.at[1])
     arrived_heads(n.l_recv, n.s_l.at[1])
 
@@ -775,6 +780,28 @@
     tt = rcopy(n.t_send, n.t_recv, n.s_tt.at[0], n.s_tt.at[1], sib)
     tt.start()
 
+    up_total = stage4_out(1)
+    up_total = jnp.concatenate([up_total[:8], up_total[8:]], axis=1)
+    for e in range(8):
+        n.f_send[e] = pltpu.roll(up_total, (256 - 20 * e) % 256, 1)[:, :128]
+
+    def f_copy(e):
+        return rcopy(n.f_send.at[e], n.f_recv.at[g], n.s_f.at[0], n.s_f.at[1], f_to(e))
+
+    f_own = lax.rem(t, 8)
+
+    def f_start(e):
+        @pl.when(jnp.logical_not(f_self & (e == f_own)))
+        def _():
+            f_copy(e).start()
+
+    each(8, f_start)
+
+    @pl.when(f_self)
+    def _():
+        n.f_recv[g] = n.f_send[f_own]
+    stage4_send(1)
+
     def o2(k):
         i = far_core(k)
         return rcopy(
@@ -796,28 +823,6 @@
     @pl.when(jnp.logical_not(relays))
     def _():
         o2(15).start()
-
-    up_total = stage4_out(1)
-    up_total = jnp.concatenate([up_total[:8], up_total[8:]], axis=1)
-    for e in range(8):
-        n.f_send[e] = pltpu.roll(up_total, (256 - 20 * e) % 256, 1)[:, :128]
-
-    def f_copy(e):
-        return rcopy(n.f_send.at[e], n.f_recv.at[g], n.s_f.at[0], n.s_f.at[1], f_to(e))
-
-    f_own = lax.rem(t, 8)
-
-    def f_start(e):
-        @pl.when(jnp.logical_not(f_self & (e == f_own)))
-        def _():
-            f_copy(e).start()
-
-    each(8, f_start)
-
-    @pl.when(f_self)
-    def _():
-        n.f_recv[g] = n.f_send[f_own]
-    stage4_send(1)
 
     def left_heads(buf, sem, more=0):
         @pl.when(relays)

time: 49.7 us -> 49 us (0.986)
  the two profiles are of different devices: /device:TPU:3 before, /device:TPU:1 now
where the time goes in v5:
time: 49 us; the launch traced here: 48.9 us
  Pallas kernels  48.3 us (99%)
  between operations  0.64 us (1%)
    pallas_call x1, Pallas kernels, body(): pl.pallas_call(kernel, out_shape=shapes, in_specs=[hbm] * 14, out_specs=(...  46.8 us
    pallas_call x1, Pallas kernels, body(): pl.pallas_call(hand_out, out_shape=shapes, in_specs=[vmem] * 3, out_specs...  1.48 us

profile of v5, /device:TPU:1, one launch (start us, length us, event | category | flops | bytes accessed | tf_op | source)
XLA Modules:
  0.0 48.9 jit_solution(17260344272142719012)
XLA Ops:
  0.6 46.8 %update_and_decode.1 = (bf16[4,4,160]{2,1,0:T(4,128)(2,1)}, f32[64,256]{1,0:T(8,128)}, f32[20,64]{1,0:T(8,128)}) custom-call(bf16[128,8192]{1,0:T(8,128)(2,1)} %hid.1, bf16[128,5120]{1,0:T(8,128)(2,1)} %cot.1, f32[64,256]{1,0:T(8,128)} %bitcast.7, f32[64,5120]{1,0:T(8,128)} %up.1, bf16[256,5120]{1,0:T(8,128)(2,1)} %wo.1, bf16[5120,256]{1,0:T(8,128)(2,1)} %wq.1, ...), custom_call_target="tpu_custom_call" | custom-call | tf_op jit(solution)/shard_map/update_and_decode/pallas_call | solution.py:933
  47.4 1.5 %hand_out.1 = (bf16[4,4,160]{2,1,0:T(4,128)(2,1)}, f32[64,256]{1,0:T(8,128)}, f32[20,64]{1,0:T(8,128)}) custom-call(bf16[4,4,160]{2,1,0:T(4,128)(2,1)} %get-tuple-element.9.dec, f32[64,256]{1,0:T(8,128)} %get-tuple-element.10.fd, f32[20,64]{1,0:T(8,128)} %get-tuple-element.11.fu), custom_call_target="tpu_custom_call" | custom-call | tf_op jit(solution)/shard_map/hand_out/pallas_call | solution.py:946

commit v6 on v4

--- a/solution.py
+++ b/solution.py
@@ -235,13 +235,14 @@
             arrived(buf, 16 + more, sem)
 
     barrier = pltpu.get_barrier_semaphore()
-    each(
-        32,
-        lambda k: pl.semaphore_signal(
+    def t_greet(k):
+        pl.semaphore_signal(
             barrier, inc=1, device_id=tdev(lax.rem(t + k, 32)), device_id_type=MESH
-        ),
-        1,
-    )
+        )
+
+    near = (1, 31, 16, 15, 17)
+    for k in near:
+        t_greet(k)
     each(
         8,
         lambda k: pl.semaphore_signal(
@@ -277,6 +278,10 @@
     @pl.when(jnp.logical_not(f_self))
     def _():
         f_greet(g)
+
+    for k in range(1, 32):
+        if k not in near:
+            t_greet(k)
 
     loads["down"].wait()
     n.down_own[...] = n.v_down[...].astype(BF16)
@@ -626,17 +631,18 @@
                 tile = jnp.where(tile_lane == 64 + r, sums[r][rows], tile)
             n.l_send[pair * 8 + j] = tile
 
-    loop(1, attend)
+    first = jnp.where(relays, 1, 0)
+    loop(first, attend)
 
     stage3_out(0)
-    send_parts(0)
+    loop(first, send_parts)
 
     until = jnp.where(relays, 2, 1)
     def attend_and_send(step):
         attend(step)
         send_parts(step)
 
-    loop(until, attend_and_send, 1)
+    loop(until, attend_and_send, first)
 
     pt.wait_recv()
     pairs[3].wait_recv()

time: 49.7 us -> 48.7 us (0.980)
  Pallas kernels: 48.9 us -> 47.9 us
    pallas_call x1, Pallas kernels: 47.4 us -> 46.4 us  [body(): pl.pallas_call(kernel, out_shape=shapes, in_specs=[hbm] * 14, out_specs=(...]
where the time goes in v6:
time: 48.7 us; the launch traced here: 48.5 us
  Pallas kernels  47.9 us (98%)
  between operations  0.64 us (1%)
    pallas_call x1, Pallas kernels, body(): pl.pallas_call(kernel, out_shape=shapes, in_specs=[hbm] * 14, out_specs=(...  46.4 us
    pallas_call x1, Pallas kernels, body(): pl.pallas_call(hand_out, out_shape=shapes, in_specs=[vmem] * 3, out_specs...  1.48 us

profile of v6, /device:TPU:3, one launch (start us, length us, event | category | flops | bytes accessed | tf_op | source)
XLA Modules:
  0.0 48.5 jit_solution(14227859881274545595)
XLA Ops:
  0.6 46.4 %update_and_decode.1 = (bf16[4,4,160]{2,1,0:T(4,128)(2,1)}, f32[64,256]{1,0:T(8,128)}, f32[20,64]{1,0:T(8,128)}) custom-call(bf16[128,8192]{1,0:T(8,128)(2,1)} %hid.1, bf16[128,5120]{1,0:T(8,128)(2,1)} %cot.1, f32[64,256]{1,0:T(8,128)} %bitcast.7, f32[64,5120]{1,0:T(8,128)} %up.1, bf16[256,5120]{1,0:T(8,128)(2,1)} %wo.1, bf16[5120,256]{1,0:T(8,128)(2,1)} %wq.1, ...), custom_call_target="tpu_custom_call" | custom-call | tf_op jit(solution)/shard_map/update_and_decode/pallas_call | solution.py:934
  47.1 1.5 %hand_out.1 = (bf16[4,4,160]{2,1,0:T(4,128)(2,1)}, f32[64,256]{1,0:T(8,128)}, f32[20,64]{1,0:T(8,128)}) custom-call(bf16[4,4,160]{2,1,0:T(4,128)(2,1)} %get-tuple-element.9.dec, f32[64,256]{1,0:T(8,128)} %get-tuple-element.10.fd, f32[20,64]{1,0:T(8,128)} %get-tuple-element.11.fu), custom_call_target="tpu_custom_call" | custom-call | tf_op jit(solution)/shard_map/hand_out/pallas_call | solution.py:947
